TPU v7x, 256 devices: a whole 4x4x8 slice. The times are simulated.
256 devices in a mesh: dp: 4 (over x), zero: 64 (over y, z, core).
Axes of the slice: x: 4, y: 4, z: 8, core: 2. Of those that a mesh axis runs over, the one named last changes fastest.
Arguments:
- hidden_in: bfloat16 [512, 4608], P(('dp', 'zero')), may hold values from -16 to 16
- targets: bfloat16 [512, 4608], P(('dp', 'zero')), may hold values from -16 to 16
- norm_gain: float32 [4608], replicated, may hold values from 0.5 to 2
- up_weight: bfloat16 [24576, 4608], P('zero'), may hold values from -0.35 to 0.35
- down_weight: bfloat16 [24576, 4608], P('zero'), may hold values from -0.0390625 to 0.0390625
- start: float32 [24576, 4608], P(('zero', 'dp')), may hold values from -24 to 24
Outputs:
- basis_next: float32 [2, 24576, 4608], P(None, ('zero', 'dp'))
- first_quotient: float32 [1], replicated
- coefficients: float32 [2, 2], replicated
All inputs are finite; a program needn't handle non-finite values.
Results may differ from a plain program's by a relative error of at most 0.017.
Values may be sent and summed in bfloat16 or wider, within the bound.
A program may use at most 128 MiB of HBM per device.

v0:
```python
import jax
import jax.numpy as jnp
from jax import lax
from jax.sharding import PartitionSpec as P

norm_eps = 1e-06
gelu_coef = 0.7978845608028654


def gelu_value(inputs):
    return (
        0.5 * inputs * (1.0 + jnp.tanh(gelu_coef * (inputs + 0.044715 * inputs * inputs * inputs)))
    )


def gelu_parts(inputs):
    unit_dir = jnp.ones_like(inputs)

    def first_slope(points):
        return jax.jvp(gelu_value, (points,), (unit_dir,))[1]

    return (
        gelu_value(inputs),
        first_slope(inputs),
        jax.jvp(first_slope, (inputs,), (unit_dir,))[1],
    )


def token_loss(branch, residual, target, norm_gain, token_count):
    summed = residual.astype(jnp.float32) + branch
    normed = summed * lax.rsqrt(jnp.mean(summed * summed, axis=-1, keepdims=True) + norm_eps)
    misfit = normed * norm_gain - target.astype(jnp.float32)
    return 0.5 * jnp.sum(misfit * misfit) / token_count


def branch_grad(branch, residual, target, norm_gain, token_count):
    return jax.grad(token_loss)(branch, residual, target, norm_gain, token_count)


def branch_curv(branch, tangent, residual, target, norm_gain, token_count):

    def inner_grad(point):
        return branch_grad(point, residual, target, norm_gain, token_count)

    return jax.jvp(inner_grad, (branch,), (tangent,))[1]


def contract_hidden(activations, weight):
    return lax.dot_general(
        activations, weight, (((1,), (1,)), ((), ())), preferred_element_type=jnp.float32
    )


def contract_tokens(factor, activations):
    return lax.dot_general(
        factor, activations, (((0,), (0,)), ((), ())), preferred_element_type=jnp.float32
    )


def summed_rows(hidden_act, down_weight):
    return lax.psum_scatter(
        jnp.dot(hidden_act, down_weight, preferred_element_type=jnp.float32),
        "zero",
        scatter_dimension=0,
        tiled=True,
    )


def spread_rows(local_rows):
    return lax.all_gather(local_rows, "zero", axis=0, tiled=True)


def orthogonalize(basis, fresh_image, entry_count):
    local_coeffs = jnp.stack([jnp.sum(member * fresh_image) for member in basis])
    coeffs = lax.psum(local_coeffs, ("dp", "zero")) / entry_count
    leftover = fresh_image
    for position, member in enumerate(basis):
        leftover = leftover - coeffs[position] * member
    spread_sq = lax.psum(jnp.sum(leftover * leftover), ("dp", "zero")) / entry_count
    return (coeffs, leftover, spread_sq)


def per_device(hidden_in, targets, norm_gain, up_weight, down_weight, start):
    tok_rows = hidden_in.shape[0]
    shard_count = lax.axis_size("dp") * lax.axis_size("zero")
    token_count = float(tok_rows * shard_count)
    entry_count = float(start.shape[0] * shard_count * start.shape[1])
    tokens = lax.all_gather(hidden_in, "zero", axis=0, tiled=True)
    pre_act = contract_hidden(tokens, up_weight)
    gelu_out, gelu_slope, gelu_bend = gelu_parts(pre_act)
    hidden_act = gelu_out.astype(jnp.bfloat16)
    branch = summed_rows(hidden_act, down_weight)
    grad_local = branch_grad(branch, hidden_in, targets, norm_gain, token_count).astype(
        jnp.bfloat16
    )
    act_grad = contract_hidden(spread_rows(grad_local), down_weight)

    def curvature(direction):
        direction_bf = direction.astype(jnp.bfloat16)
        whole_dir = lax.all_gather(direction_bf, "dp", axis=0, tiled=True)
        pre_tangent = contract_hidden(tokens, whole_dir)
        act_tangent = (gelu_slope * pre_tangent).astype(jnp.bfloat16)
        branch_tangent = summed_rows(act_tangent, down_weight)
        grad_tangent = branch_curv(
            branch, branch_tangent, hidden_in, targets, norm_gain, token_count
        ).astype(jnp.bfloat16)
        act_grad_tangent = contract_hidden(spread_rows(grad_tangent), down_weight)
        pre_grad_tangent = (
            act_grad_tangent * gelu_slope + act_grad * gelu_bend * pre_tangent
        ).astype(jnp.bfloat16)
        return lax.psum_scatter(
            contract_tokens(pre_grad_tangent, tokens).astype(jnp.bfloat16),
            "dp",
            scatter_dimension=0,
            tiled=True,
        ).astype(jnp.float32)

    start_square = lax.psum(jnp.sum(start * start), ("dp", "zero")) / entry_count
    first_vec = start * lax.rsqrt(start_square + norm_eps)
    image_one = curvature(first_vec)
    coeffs_one, left_one, square_one = orthogonalize([first_vec], image_one, entry_count)
    scale_two = lax.rsqrt(square_one + norm_eps)
    second_vec = left_one * scale_two
    image_two = curvature(second_vec)
    coeffs_two, left_two, square_two = orthogonalize(
        [first_vec, second_vec], image_two, entry_count
    )
    third_vec = left_two * lax.rsqrt(square_two + norm_eps)
    coefficients = jnp.stack(
        [
            jnp.stack([coeffs_two[0], coeffs_two[1]]),
            jnp.stack([jnp.sqrt(square_one), jnp.sqrt(square_two)]),
        ]
    )
    return (jnp.stack([second_vec, third_vec]), jnp.reshape(coeffs_one[0], (1,)), coefficients)


def solution(mesh):
    placed = (
        P(("dp", "zero"), None),
        P(("dp", "zero"), None),
        P(),
        P("zero", None),
        P("zero", None),
        P(("zero", "dp"), None),
    )
    return jax.shard_map(
        per_device,
        mesh=mesh,
        in_specs=placed,
        out_specs=(P(None, ("zero", "dp"), None), P(), P()),
        check_vma=False,
    )
```

profile of v0, /device:TPU:1, one launch (start us, length us, event | category | flops | bytes accessed | tf_op | source)
XLA Modules:
  0.0 1253.5 jit_solution(12082300233608745532)
XLA Ops:
  7.2 0.7 all-gather.15.cloned.1.call-update
  8.0 2.8 multiply_reduce_fusion.2
  10.8 81.7 %psum.35 = f32[]{:T(128)} all-reduce(f32[]{:T(128)} %multiply_reduce_fusion.2), channel_id=1, replica_groups=mesh['dp'=4,'zero'=64] {'dp','zero'}, use_global_device_ids=true, to_apply=%region_1.0 | all-reduce | flops 1 | bytes 8 | tf_op jit(solution)/shard_map/psum | solution.py:118
  93.2 2.5 multiply_convert_fusion.1
  95.8 2.3 reshape.78
  98.1 3.5 fusion.45
  101.7 0.7 copy-done.1
  102.4 2.2 fusion.22
  104.6 32.2 %all-gather.11.cloned.1.call-done = bf16[384,4608]{1,0:T(8,128)(2,1)} async-done(((bf16[96,4608]{1,0:T(8,128)(2,1)}), bf16[384,4608]{1,0:T(8,128)(2,1)}) %all-gather.11.cloned.1.call-update) | async-done | bytes 3538960 | tf_op jit(solution)/shard_map/all_gather | solution.py:100
  136.8 3.6 convolution_bitcast_fusion.1
  140.4 0.7 copy-done.4
  141.0 2.3 fusion.21
  145.2 1.3 broadcast_multiply_fusion
  146.6 192.3 %all-reduce.9.cloned.1.call-done = (f32[128,4608]{1,0:T(8,128)}, f32[128,4608]{1,0:T(8,128)}) async-done(((f32[128,4608]{1,0:T(8,128)}, f32[128,4608]{1,0:T(8,128)}), (f32[128,4608]{1,0:T(8,128)}, f32[128,4608]{1,0:T(8,128)})) %all-reduce.9.cloned.1.call-update) | async-done | bytes 4718608
  338.9 1.2 multiply_reduce_fusion.4
  340.1 1.2 add_reduce_fusion.1
  341.4 1.8 fusion.31
  343.8 76.7 %all-gather.19.cloned.1.call-done = bf16[64,2,4608]{2,1,0:T(2,128)(2,1)} async-done(((bf16[1,2,4608]{2,1,0:T(2,128)(2,1)}), bf16[64,2,4608]{2,1,0:T(2,128)(2,1)}) %all-gather.19.cloned.1.call-update) | async-done | bytes 1179664 | tf_op jit(solution)/shard_map/all_gather | solution.py:70
  420.5 2.3 reshape.82
  422.9 3.2 convolution_multiply_fusion.1
  426.0 71.6 %all-gather.17.cloned.1.call-done = bf16[64,2,4608]{2,1,0:T(2,128)(2,1)} async-done(((bf16[1,2,4608]{2,1,0:T(2,128)(2,1)}), bf16[64,2,4608]{2,1,0:T(2,128)(2,1)}) %all-gather.17.cloned.1.call-update) | async-done | bytes 1179664 | tf_op jit(solution)/shard_map/all_gather | solution.py:70
  497.7 2.4 reshape.80
  500.0 6.5 convolution_convert_fusion.1
  506.6 41.5 %reduce-scatter.3.cloned.1.call-done = bf16[96,4608]{1,0:T(8,128)(2,1)} async-done(((bf16[384,4608]{1,0:T(8,128)(2,1)}), bf16[96,4608]{1,0:T(8,128)(2,1)}) %reduce-scatter.3.cloned.1.call-update) | async-done | bytes 884752 | tf_op jit(solution)/shard_map/reduce_scatter | solution.py:111
  548.0 2.8 fusion
  550.9 75.9 %psum.36 = f32[1]{0:T(128)} all-reduce(f32[1]{0:T(128)} %bitcast.4), channel_id=1, replica_groups=mesh['dp'=4,'zero'=64] {'dp','zero'}, use_global_device_ids=true, to_apply=%region_10.0 | all-reduce | flops 1 | bytes 8 | tf_op jit(solution)/shard_map/psum | solution.py:75
  627.4 2.8 multiply_reduce_fusion.1
  630.2 74.3 %psum.37 = f32[]{:T(128)} all-reduce(f32[]{:T(128)} %multiply_reduce_fusion.1), channel_id=1, replica_groups=mesh['dp'=4,'zero'=64] {'dp','zero'}, use_global_device_ids=true, to_apply=%region_12.0 | all-reduce | flops 1 | bytes 8 | tf_op jit(solution)/shard_map/psum | solution.py:79
  705.2 2.9 multiply_convert_fusion
  708.4 41.5 %all-gather.13.cloned.1.call-done = bf16[384,4608]{1,0:T(8,128)(2,1)} async-done(((bf16[96,4608]{1,0:T(8,128)(2,1)}), bf16[384,4608]{1,0:T(8,128)(2,1)}) %all-gather.13.cloned.1.call-update) | async-done | bytes 3538960 | tf_op jit(solution)/shard_map/all_gather | solution.py:100
  749.9 3.6 convolution_bitcast_fusion
  753.4 0.7 copy-done.5
  754.1 2.3 fusion.23
  756.4 189.0 %all-reduce.7.cloned.1.call-done = f32[128,4608]{1,0:T(8,128)} async-done(((f32[128,4608]{1,0:T(8,128)}), f32[128,4608]{1,0:T(8,128)}) %all-reduce.7.cloned.1.call-update) | async-done | bytes 2359312
  945.5 1.1 multiply_reduce_fusion.3
  947.2 1.2 add_reduce_fusion
  949.0 1.7 fusion.32
  950.8 77.4 %all-gather.21.cloned.1.call-done = bf16[64,2,4608]{2,1,0:T(2,128)(2,1)} async-done(((bf16[1,2,4608]{2,1,0:T(2,128)(2,1)}), bf16[64,2,4608]{2,1,0:T(2,128)(2,1)}) %all-gather.21.cloned.1.call-update) | async-done | bytes 1179664 | tf_op jit(solution)/shard_map/all_gather | solution.py:70
  1028.1 2.3 reshape.84
  1030.5 6.5 convolution_convert_fusion
  1037.0 41.5 %reduce-scatter.5.cloned.1.call-done = bf16[96,4608]{1,0:T(8,128)(2,1)} async-done(((bf16[384,4608]{1,0:T(8,128)(2,1)}), bf16[96,4608]{1,0:T(8,128)(2,1)}) %reduce-scatter.5.cloned.1.call-update) | async-done | bytes 884752 | tf_op jit(solution)/shard_map/reduce_scatter | solution.py:111
  1078.5 3.1 fusion.1
  1081.6 1.4 pad_maximum_fusion.2
  1083.0 76.0 %psum.38 = f32[2]{0:T(128)S(1)} all-reduce(f32[2]{0:T(128)S(1)} %pad_maximum_fusion.2), channel_id=1, replica_groups=mesh['dp'=4,'zero'=64] {'dp','zero'}, use_global_device_ids=true, to_apply=%region_19.0 | all-reduce | flops 2 | bytes 16 | tf_op jit(solution)/shard_map/psum | solution.py:75
  1159.5 4.5 multiply_reduce_fusion
  1164.0 74.3 %psum.39 = f32[]{:T(128)} all-reduce(f32[]{:T(128)} %multiply_reduce_fusion), channel_id=1, replica_groups=mesh['dp'=4,'zero'=64] {'dp','zero'}, use_global_device_ids=true, to_apply=%region_21.0 | all-reduce | flops 1 | bytes 8 | tf_op jit(solution)/shard_map/psum | solution.py:79
  1239.7 3.8 multiply_bitcast_fusion.1
  1243.5 2.0 pad_maximum_fusion
  (44 shorter events, 5.0 us)
Async XLA Ops:
  7.2 95.2 %copy-start = (bf16[384,4608]{1,0:T(8,128)(2,1)S(1)}, bf16[384,4608]{1,0:T(8,128)(2,1)}, u32[]{:S(2)}) copy-start(bf16[384,4608]{1,0:T(8,128)(2,1)} %param.10) | copy-start | bytes 10616836
  7.2 88.6 %all-gather.15.cloned.1.call-start = ((), (), s32[]{:S(2)}) async-start(), calls=%async_computation.6 | async-start | bytes 1198080 | tf_op jit(solution)/shard_map/all_gather | solution.py:88
  7.9 128.9 %all-gather.11.cloned.1.call-start = ((), (), s32[]{:S(2)}) async-start(), calls=%async_computation.2 | async-start | bytes 4423680 | tf_op jit(solution)/shard_map/all_gather | solution.py:100
  95.7 243.2 %all-reduce.9.cloned.1.call-start = ((), (), s32[]{:S(2)}) async-start(), calls=%async_computation.11 | async-start | bytes 9437184
  101.6 0.7 copy-start.1
  136.8 4.2 copy-start.2
  140.3 0.7 copy-start.4
  143.3 0.7 copy-start.8
  143.3 277.2 %all-gather.19.cloned.1.call-start = ((), (), s32[]{:S(2)}) async-start(), calls=%async_computation.8 | async-start | bytes 1198080 | tf_op jit(solution)/shard_map/all_gather | solution.py:70
  340.1 1.3 copy-start.6
  340.1 3.1 copy-start.7
  343.2 154.5 %all-gather.17.cloned.1.call-start = ((), (), s32[]{:S(2)}) async-start(), calls=%async_computation.7 | async-start | bytes 1198080 | tf_op jit(solution)/shard_map/all_gather | solution.py:70
  343.8 204.3 %reduce-scatter.3.cloned.1.call-start = ((), (), s32[]{:S(2)}) async-start(), calls=%async_computation.3 | async-start | bytes 4423680 | tf_op jit(solution)/shard_map/reduce_scatter | solution.py:111
  506.5 243.3 %all-gather.13.cloned.1.call-start = ((), (), s32[]{:S(2)}) async-start(), calls=%async_computation.4 | async-start | bytes 4423680 | tf_op jit(solution)/shard_map/all_gather | solution.py:100
  708.1 237.3 %all-reduce.7.cloned.1.call-start = ((), (), s32[]{:S(2)}) async-start(), calls=%async_computation.10 | async-start | bytes 4718592
  749.9 4.2 copy-start.3
  753.4 0.7 copy-start.5
  756.4 271.7 %all-gather.21.cloned.1.call-start = ((), (), s32[]{:S(2)}) async-start(), calls=%async_computation.9 | async-start | bytes 1198080 | tf_op jit(solution)/shard_map/all_gather | solution.py:70
  950.7 127.8 %reduce-scatter.5.cloned.1.call-start = ((), (), s32[]{:S(2)}) async-start(), calls=%async_computation.5 | async-start | bytes 4423680 | tf_op jit(solution)/shard_map/reduce_scatter | solution.py:111
Sparse Core Ops, SparseCore 0:
  10.7 80.6 all-gather.14
  95.8 40.9 all-gather.10
  143.5 195.3 all-reduce.8
  343.3 77.1 all-gather.18
  423.4 74.2 all-gather.16
  506.7 41.3 reduce-scatter.2
  708.2 41.5 all-gather.12
  756.5 188.9 all-reduce.6
  950.8 77.2 all-gather.20
  1037.1 41.3 reduce-scatter.4
where the time goes:
time: 1250 us
  waiting for transfers between devices  765 us (61%)
  blocking collectives  382 us (31%)
  other arithmetic  40.1 us (3%)
  matrix products  33.6 us (3%)
  between operations  18.9 us (2%)
  local copies, waits for them, and re-layouts  13.2 us (1%)
    unnamed x12, waiting for transfers between devices  383 us
    all_gather x3, waiting for transfers between devices, spread_rows(): return lax.all_gather(local_rows, 'zero', axis=0, tiled=True)  226 us
    psum x2, blocking collectives, orthogonalize(): coeffs = lax.psum(local_coeffs, ('dp', 'zero')) / entry_count  152 us
    psum x2, blocking collectives, orthogonalize(): lax.psum(jnp.sum(leftover * leftover), ('dp', 'zero')) / entry_count  149 us
    reduce_scatter x2, waiting for transfers between devices, curvature(): lax.psum_scatter(contract_tokens(pre_grad_tangent, tokens).astype(jnp.bfl...  82.9 us
    psum x1, blocking collectives, per_device(): lax.psum(jnp.sum(start * start), ('dp', 'zero')) / entry_count  81.7 us
    all_gather x2, waiting for transfers between devices, curvature(): whole_dir = lax.all_gather(direction_bf, 'dp', axis=0, tiled=True)  73.7 us
  transfers between devices with their start and end apart: 10, of which 9 were waited for; matrix products, arithmetic and copies ran while one was open for 2% of the time, Pallas kernels for 0%

commit v1 on v0

v1 whole, which is shorter than its diff:
```python
import jax
import jax.numpy as jnp
from jax import lax
from jax.experimental import pallas as pl
from jax.experimental.pallas import tpu as pltpu
from jax.sharding import PartitionSpec as P

MESH = pl.DeviceIdType.MESH
f32, bf16 = jnp.float32, jnp.bfloat16
norm_eps = 1e-06
gelu_coef = 0.7978845608028654

N_X, N_Y, N_Z, N_C = 4, 4, 8, 2
D = 4608
ROWS = 96
PAD = 128
HID = N_X * PAD
GRP = 128
TOK = N_X * GRP
HALF = GRP // N_C
BLK = HALF // N_Y
OWN = BLK // N_Z
CHUNKS = 2
W = D // CHUNKS
PIECE = 16
XA = 2560


def gelu_value(inputs):
    return (
        0.5 * inputs * (1.0 + jnp.tanh(gelu_coef * (inputs + 0.044715 * inputs * inputs * inputs)))
    )


def gelu_parts(inputs):
    unit_dir = jnp.ones_like(inputs)

    def first_slope(points):
        return jax.jvp(gelu_value, (points,), (unit_dir,))[1]

    return (
        gelu_value(inputs),
        first_slope(inputs),
        jax.jvp(first_slope, (inputs,), (unit_dir,))[1],
    )


def loss_parts(summed, target, gain):
    r = lax.rsqrt(jnp.sum(summed * summed, axis=-1, keepdims=True) / D + norm_eps)
    normed = summed * r
    pull = (normed * gain - target) * gain
    mean = jnp.sum(pull * normed, axis=-1, keepdims=True) / D
    return r, normed, pull, mean


def loss_grad(summed, target, gain):
    r, normed, pull, mean = loss_parts(summed, target, gain)
    return r * (pull - normed * mean) / float(TOK)


def loss_curv(summed, tangent, target, gain):
    r, normed, pull, mean = loss_parts(summed, target, gain)
    along = jnp.sum(normed * tangent, axis=-1, keepdims=True) / D
    d_normed = r * (tangent - normed * along)
    d_pull = d_normed * gain * gain
    d_mean = jnp.sum(d_pull * normed + pull * d_normed, axis=-1, keepdims=True) / D
    grad = r * (pull - normed * mean)
    d_grad = r * (d_pull - d_normed * mean - normed * d_mean) - (r * along) * grad
    return d_grad / float(TOK)


def dot_t(a, b):
    return lax.dot_general(a, b, (((1,), (1,)), ((), ())), preferred_element_type=f32)


def dot(a, b):
    return jnp.dot(a, b, preferred_element_type=f32)


def tile_sum(v):
    rows, cols = v.shape
    acc = v[0:8, :]
    for i in range(8, rows, 8):
        acc = acc + v[i : i + 8, :]
    out = acc[:, 0:128]
    for k in range(128, cols, 128):
        out = out + acc[:, k : k + 128]
    return out


def par(*gens):
    gens = list(gens)
    while gens:
        for g in list(gens):
            try:
                next(g)
            except StopIteration:
                gens.remove(g)
        if gens:
            yield


def run(*gens):
    for _ in par(*gens):
        pass


def play(gens, order):
    for j in order:
        next(gens[j], None)
    run(*gens)


def kernel(
    hin, tgt, gain, up_hbm, down_hbm, start_hbm,
    kw_hbm, k2_hbm, mix,
    up, down, start, sbf, X, xz, tmp16, part,
    sb, rc, s1f, y1b, y1r, y2b, y2r, sz, rz, az, A,
    slope, bendag, hact, agrad, pt1, ptx, pts, ptr,
    pfull, pr2, gram, kw, k2, arv, arr, tot, bsum,
    ld_sem, xz_s, xz_r, xy_s, xy_r, xc_s, xc_r,
    xa_s, xa_r, xac_s, xac_r, xb_s, xb_r, xby_s, xby_r, xbc_s, xbc_r,
    rc_s, rc_r, y1_s, y1_r, y2_s, y2_r, rz_s, rz_r,
    az_s, az_r, ay_s, ay_r, ac_s, ac_r,
    pt_s, pt_r, pf_s, pf_r, p2_s, p2_r, ar_s, ar_r, out_sem,
):
    x = lax.axis_index("dp")
    shard = lax.axis_index("zero")
    y, z, c = shard // 16, (shard // 2) % 8, shard % 2

    def dev(nx, ny, nz, nc):
        return (nx, ny * 16 + nz * 2 + nc)

    def x_at(k):
        return (x + (k % N_X)) % N_X

    def y_at(k):
        return (y + (k % N_Y)) % N_Y

    def x_peer(k):
        return dev(x_at(k), y, z, c)

    def y_peer(k):
        return dev(x, y_at(k), z, c)

    def z_peer(k):
        return dev(x, y, (z + k) % N_Z, c)

    c_peer = dev(x, y, z, 1 - c)

    def xy_peer(k):
        return dev(x_at(k // N_Y), y_at(k % N_Y), z, c)

    def zc_peer(k):
        return dev(x, y, (z + k // N_C) % N_Z, (c + k % N_C) % N_C)

    def send(src, dst, ssem, rsem, to):
        cp = pltpu.make_async_remote_copy(
            src_ref=src, dst_ref=dst, send_sem=ssem, recv_sem=rsem, device_id=to, device_id_type=MESH
        )
        cp.start()
        return cp

    def rows(start_row, count):
        return pl.ds(pl.multiple_of(start_row, 16), count)

    def wait_all(cps):
        for cp in cps:
            cp.wait()

    loads = []
    for b in range(N_X):
        for j, (src, dst) in enumerate(((up_hbm, up), (down_hbm, down))):
            loads.append(
                pltpu.make_async_copy(
                    src.at[pl.ds(b * ROWS, ROWS)], dst.at[pl.ds(b * PAD, ROWS)], ld_sem.at[2 * b + j]
                )
            )
    loads.append(pltpu.make_async_copy(start_hbm, start, ld_sem.at[2 * N_X]))
    for cp in loads:
        cp.start()

    barrier = pltpu.get_barrier_semaphore()
    peers = [xy_peer(k) for k in range(1, N_X * N_Y)] + [zc_peer(k) for k in range(1, N_Z * N_C)]
    for p in peers:
        pl.semaphore_signal(barrier, inc=1, device_id=p, device_id_type=MESH)
    pl.semaphore_wait(barrier, len(peers))

    def ring_gather(ref, blocks, c0, w, peer, ssem, rsem, then=None):
        half = w // 2
        nb = len(blocks)
        first = []
        for b, (row_of, count) in enumerate(blocks):
            at = (rows(row_of(0), count), pl.ds(c0, w))
            first.append(
                [
                    send(ref.at[at], ref.at[at], ssem.at[2 * b + j], rsem.at[2 * b + j], peer(to))
                    for j, to in enumerate((1, -1))
                ]
            )
        if then:
            then(0)
        yield
        second = []
        for b, (row_of, count) in enumerate(blocks):
            for j, to in enumerate((1, -1)):
                first[b][j].wait()
                at = (rows(row_of(-to), count), pl.ds(c0 + j * half, half))
                i = 2 * (nb + b) + j
                second.append(send(ref.at[at], ref.at[at], ssem.at[i], rsem.at[i], peer(to)))
        if then:
            then(-1)
            then(1)
        yield
        wait_all(second)
        if then:
            then(2)

    def gather_z(own, buf, ssem, rsem):
        buf[z] = own
        return [
            send(buf.at[z], buf.at[z], ssem.at[k - 1], rsem.at[k - 1], z_peer(k)) for k in range(1, N_Z)
        ]

    def join16(buf, c0, w):
        for j in range(N_Z):
            tmp16[pl.ds(OWN * j, OWN), c0 : c0 + w] = buf[j].astype(f32)
        return tmp16[:, c0 : c0 + w].astype(bf16)

    def gather(own, i, h):
        c0, out = h * W, A.at[i]
        cols = pl.ds(c0, W)
        cps = gather_z(own[:, c0 : c0 + W], az.at[i, h], az_s.at[i, h], az_r.at[i, h])
        yield
        wait_all(cps)
        out[rows(c * HALF + y * BLK, BLK), cols] = join16(az.at[i, h], c0, W)
        passed = []

        def pass_on(k):
            at = (rows(c * HALF + y_at(k) * BLK, BLK), cols)
            passed.append(send(out.at[at], out.at[at], ac_s.at[i, h, k % 4], ac_r.at[i, h, k % 4], c_peer))

        yield from ring_gather(
            out,
            [(lambda k: c * HALF + y_at(k) * BLK, BLK)],
            c0,
            W,
            y_peer,
            ay_s.at[i, h],
            ay_r.at[i, h],
            pass_on,
        )
        yield
        wait_all(passed)
        part_grad = dot_t(out[:, cols], down[:, cols])
        if h == 0:
            agrad[i % 2] = part_grad
        else:
            agrad[i % 2] = agrad[i % 2] + part_grad

    def scatter(i, h, make=None):
        c0 = h * W
        cols = slice(c0, c0 + W)
        if make is not None:
            make(h)
        sb[i, h] = part[rows((1 - c) * HALF, HALF), cols].astype(bf16)
        cps = [send(sb.at[i, h], rc.at[i, h], rc_s.at[i, h], rc_r.at[i, h], c_peer)]
        yield
        wait_all(cps)
        s1f[i % 2, :, cols] = part[rows(c * HALF, HALF), cols] + rc[i, h].astype(f32)

        def block(k):
            return s1f[i % 2, rows(y_at(k) * BLK, BLK), cols]

        half = W // 2
        y1b[i, h] = block(2).astype(bf16)
        cps = [
            send(
                y1b.at[i, h, :, pl.ds(j * half, half)],
                y1r.at[i, h, :, pl.ds(j * half, half)],
                y1_s.at[i, h, j],
                y1_r.at[i, h, j],
                y_peer(to),
            )
            for j, to in enumerate((1, -1))
        ]
        yield
        wait_all(cps)
        got = y1r[i, h].astype(f32)
        for j, to in enumerate((1, -1)):
            mine = block(to)
            if j == 0:
                pieces = [mine[:, :half] + got[:, :half], mine[:, half:]]
            else:
                pieces = [mine[:, :half], mine[:, half:] + got[:, half:]]
            y2b[i, h, j, :, pl.ds(0, half)] = pieces[0].astype(bf16)
            y2b[i, h, j, :, pl.ds(half, half)] = pieces[1].astype(bf16)
        cps = [
            send(y2b.at[i, h, j], y2r.at[i, h, j], y2_s.at[i, h, j], y2_r.at[i, h, j], y_peer(to))
            for j, to in enumerate((1, -1))
        ]
        yield
        wait_all(cps)
        tmp16[:, cols] = block(0) + y2r[i, h, 0].astype(f32) + y2r[i, h, 1].astype(f32)
        for j in range(N_Z):
            sz[i, h, j] = tmp16[pl.ds(OWN * j, OWN), cols].astype(bf16)
        cps = [
            send(
                sz.at[i, h, (z + k) % N_Z],
                rz.at[i, h, k - 1],
                rz_s.at[i, h, k - 1],
                rz_r.at[i, h, k - 1],
                z_peer(k),
            )
            for k in range(1, N_Z)
        ]
        yield
        wait_all(cps)
        s3 = sz[i, h, z].astype(f32)
        for k in range(N_Z - 1):
            s3 = s3 + rz[i, h, k].astype(f32)
        tot[i, :, cols] = s3

    def scatters(i, make):
        return par(*[scatter(i, h, make) for h in range(CHUNKS)])

    def gathers(own, i):
        return par(*[gather(own, i, h) for h in range(CHUNKS)])

    def all_sum(i, n):
        for s, peer in enumerate((xy_peer, zc_peer)):
            cps = [
                send(
                    arv.at[i, s, pl.ds(0, n)],
                    arr.at[i, s, k - 1, pl.ds(0, n)],
                    ar_s.at[i, s, k - 1],
                    ar_r.at[i, s, k - 1],
                    peer(k),
                )
                for k in range(1, 16)
            ]
            yield
            wait_all(cps)
            acc = arv[i, s, 0:n]
            for k in range(1, 16):
                acc = acc + arr[i, s, k - 1, 0:n]
            arv[i, s + 1, 0:n] = acc

    group = rows(x * GRP, GRP)

    def group_tokens(h):
        c0 = h * W
        cols = pl.ds(c0, W)
        cps = gather_z(hin[:, c0 : c0 + W], xz.at[h], xz_s.at[h], xz_r.at[h])
        yield
        wait_all(cps)
        X[rows(x * GRP + c * HALF + y * BLK, BLK), cols] = join16(xz.at[h], c0, W)
        passed = []

        def pass_on(k):
            at = (rows(x * GRP + c * HALF + y_at(k) * BLK, BLK), cols)
            passed.append(send(X.at[at], X.at[at], xc_s.at[h, k % 4], xc_r.at[h, k % 4], c_peer))

        yield from ring_gather(
            X,
            [(lambda k: x * GRP + c * HALF + y_at(k) * BLK, BLK)],
            c0,
            W,
            y_peer,
            xy_s.at[h],
            xy_r.at[h],
            pass_on,
        )
        yield
        wait_all(passed)
        pre = dot_t(X[group, cols], up[:, cols])
        if h == 0:
            agrad[0] = pre
        else:
            agrad[0] = agrad[0] + pre

    def local_work():
        for b in range(N_X):
            up[pl.ds(b * PAD + ROWS, PAD - ROWS), :] = jnp.zeros((PAD - ROWS, D), bf16)
            down[pl.ds(b * PAD + ROWS, PAD - ROWS), :] = jnp.zeros((PAD - ROWS, D), bf16)
        sbf[pl.ds(ROWS, PAD - ROWS), :] = jnp.zeros((PAD - ROWS, D), bf16)
        yield
        for cp in loads:
            cp.wait()
        sbf[pl.ds(0, ROWS), :] = start[...].astype(bf16)
        yield
        arv[0, 0, 1] = tile_sum(start[...] * start[...])

    own_xb = ring_gather(
        X, [(lambda k: x_at(k) * GRP + c * HALF + y * BLK, BLK)], XA, D - XA, x_peer, xb_s, xb_r
    )
    tok_gens = [group_tokens(h) for h in range(CHUNKS)]

    def later_xb():
        for _ in range(2):
            next(own_xb)
            yield

    both = list(range(CHUNKS))
    n = CHUNKS
    play(tok_gens + [local_work(), later_xb()], both + [n] + both + [n + 1, n] + both + [n + 1, n] + both)

    def tokens_yx():
        passed = []

        def pass_on(k):
            if k != 0:
                at = (rows(x_at(k) * GRP + c * HALF, HALF), pl.ds(0, XA))
                passed.append(send(X.at[at], X.at[at], xac_s.at[k % 4], xac_r.at[k % 4], c_peer))

        yield from ring_gather(
            X, [(lambda k: x_at(k) * GRP + c * HALF, HALF)], 0, XA, x_peer, xa_s, xa_r, pass_on
        )
        yield
        wait_all(passed)

    def tokens_xy():
        next(own_xb, None)
        blocks = [
            (lambda k, b=b: x_at(b) * GRP + c * HALF + y_at(k) * BLK, BLK) for b in range(1, N_X)
        ]
        yield from ring_gather(X, blocks, XA, D - XA, y_peer, xby_s, xby_r)
        passed = []
        for b in range(1, N_X):
            at = (rows(x_at(b) * GRP + c * HALF, HALF), pl.ds(XA, D - XA))
            passed.append(send(X.at[at], X.at[at], xbc_s.at[b], xbc_r.at[b], c_peer))
        yield
        wait_all(passed)

    def to_branch(h):
        for k in range(h * W, (h + 1) * W, W // 3):
            part[:, k : k + W // 3] = dot(hact[...], down[:, k : k + W // 3])

    def weights():
        return tgt[...].astype(f32), gain[...]

    def forward():
        for b in range(N_X):
            cols = pl.ds(b * PAD, PAD)
            value, first, second = gelu_parts(agrad[0, :, cols])
            hact[:, cols] = value.astype(bf16)
            slope[:, cols] = first
            bendag[:, cols] = second
        yield from scatters(0, to_branch)
        bsum[...] = hin[...].astype(f32) + tot[0]
        yield from gathers(loss_grad(bsum[...], *weights()).astype(bf16), 0)
        bendag[...] = bendag[...] * agrad[0]

    def first_tangent():
        pts[...] = dot_t(X[...], sbf[...])
        ptr[x] = pts[group, :]
        cps = [
            send(
                pts.at[rows(x_at(k) * GRP, GRP)], ptr.at[x], pt_s.at[k - 1], pt_r.at[k - 1], x_peer(k)
            )
            for k in range(1, N_X)
        ]
        yield
        wait_all(cps)
        for b in range(N_X):
            cols = pl.ds(b * PAD, PAD)
            pt1[:, cols] = ptr[b]
            hact[:, cols] = (slope[:, cols] * ptr[b]).astype(bf16)
        yield from scatters(1, to_branch)

    fwd = forward()
    yx, xy = tokens_yx(), tokens_xy()
    for g in (yx, xy, fwd, xy, fwd, xy, fwd, yx, fwd, yx, fwd, xy, yx):
        next(g, None)
    run(xy, yx)
    play((first_tangent(), fwd), (0, 1, 0, 1))
    curv = loss_curv(bsum[...], tot[1], *weights())

    def token_gram():
        half = TOK // 2
        for b in range(2):
            gram[:, pl.ds(b * half, half)] = dot_t(X[group, :], X[pl.ds(b * half, half), :])
            yield

    run(gathers(curv.astype(bf16), 1), token_gram())
    p1 = agrad[1] * slope[...] + bendag[...] * pt1[...]
    pfull[group, :] = p1.astype(bf16)

    def share_p1():
        yield from ring_gather(pfull, [(lambda k: x_at(k) * GRP, GRP)], 0, HID, x_peer, pf_s, pf_r)

    def own_sums():
        arv[0, 0, 0] = tile_sum(p1 * pt1[...])
        yield

    run(share_p1(), own_sums())

    g = gram[...]
    g_hi = g.astype(bf16)
    g_lo = (g - g_hi.astype(f32)).astype(bf16)
    ptx[...] = dot(g_hi, pfull[...]) + dot(g_lo, pfull[...])
    hact[...] = (slope[...] * ptx[...]).astype(bf16)

    def image_one():
        own = pfull[:, pl.ds(pl.multiple_of(x * PAD, PAD), PAD)].T
        for k in range(0, D, 512):
            kw[:, k : k + 512] = dot(own, X[:, k : k + 512])[0:ROWS, :]
            if k % 1536 == 1024:
                yield

    run(scatters(2, to_branch), all_sum(0, 2), image_one())
    count = float(ROWS * 256 * D)
    q = jnp.sum(arv[0, 2, 0], keepdims=True) / count
    ss = jnp.sum(arv[0, 2, 1], keepdims=True) / count
    s1 = lax.rsqrt(ss + norm_eps)
    h11 = s1 * s1 * q
    curv = loss_curv(bsum[...], tot[2] - h11 * tot[1], *weights())

    def remainder():
        ptx[...] = ptx[...] - h11 * pt1[...]
        acc = None
        for k in range(0, D, 1536):
            w = kw[:, k : k + 1536] - h11 * start[:, k : k + 1536]
            kw[:, k : k + 1536] = w
            s = tile_sum(w * w)
            acc = s if acc is None else acc + s
            yield
        arv[1, 0, 0] = acc

    run(gathers(curv.astype(bf16), 2), remainder())
    out_w = pltpu.make_async_copy(kw, kw_hbm, out_sem.at[0])
    out_w.start()
    for b in range(N_X):
        cols = pl.ds(b * PAD, PAD)
        pr2[1, b] = (agrad[0, :, cols] * slope[:, cols] + bendag[:, cols] * ptx[:, cols]).astype(bf16)
    pr2[0, x] = pr2[1, x]
    cps = [
        send(pr2.at[1, x_at(k)], pr2.at[0, x], p2_s.at[k - 1], p2_r.at[k - 1], x_peer(k))
        for k in range(1, N_X)
    ]
    wait_all(cps)
    sums = [None, None, None]
    for k in range(0, D, 512):
        cols = slice(k, k + 512)
        acc = None
        for b in range(N_X):
            term = dot(pr2[0, b].T, X[pl.ds(b * GRP, GRP), cols])
            acc = term if acc is None else acc + term
        acc = acc[0:ROWS, :]
        k2[:, cols] = acc
        for j, other in enumerate((start[:, cols], kw[:, cols], acc)):
            s = tile_sum(other * acc)
            sums[j] = s if sums[j] is None else sums[j] + s
    for j in range(3):
        arv[1, 0, 1 + j] = sums[j]
    out_2 = pltpu.make_async_copy(k2, k2_hbm, out_sem.at[1])
    out_2.start()
    run(all_sum(1, 4))
    ww, sk, wk, kk = [jnp.sum(arv[1, 2, j], keepdims=True) / count for j in range(4)]
    sq1 = s1 * s1 * ww
    scale2 = lax.rsqrt(sq1 + norm_eps)
    s2 = scale2 * s1
    h12 = s1 * s2 * sk
    h22 = s2 * s2 * wk
    cross = s1 * s2 * (q - h11 * ss)
    sq2 = (
        s2 * s2 * kk
        - 2.0 * (h12 * h12 + h22 * h22)
        + h12 * h12 * (s1 * s1 * ss)
        + h22 * h22 * (s2 * s2 * ww)
        + 2.0 * h12 * h22 * cross
    )
    sq2 = jnp.maximum(sq2, 0.0)
    s3 = lax.rsqrt(sq2 + norm_eps)
    results = (h11, h12, h22, jnp.sqrt(sq1), jnp.sqrt(sq2), s2, s3 * s2, -s3 * h12 * s1, -s3 * h22 * s2)
    for j, value in enumerate(results):
        mix[j] = value[0, 0]
    out_w.wait()
    out_2.wait()


def combine(mix, kw_hbm, k2_hbm, start_hbm, basis_hbm, quot, coef, kw, k2, start, out, in_sem, out_sem):
    parts = [pl.ds(r, PIECE) for r in range(0, ROWS, PIECE)]
    ins = [
        [
            pltpu.make_async_copy(src.at[at], dst.at[at], in_sem.at[j, p])
            for j, (src, dst) in enumerate(((kw_hbm, kw), (k2_hbm, k2), (start_hbm, start)))
        ]
        for p, at in enumerate(parts)
    ]
    for cps in ins:
        for cp in cps:
            cp.start()
    quot[0] = mix[0]
    coef[0, 0] = mix[1]
    coef[0, 1] = mix[2]
    coef[1, 0] = mix[3]
    coef[1, 1] = mix[4]
    outs = []
    for p, at in enumerate(parts):
        for cp in ins[p]:
            cp.wait()
        w = kw[at, :]
        out[0, at, :] = mix[5] * w
        out[1, at, :] = mix[6] * k2[at, :] + mix[7] * start[at, :] + mix[8] * w
        for j in range(2):
            cp = pltpu.make_async_copy(out.at[j, at], basis_hbm.at[j, at], out_sem.at[j, p])
            cp.start()
            outs.append(cp)
    for cp in outs:
        cp.wait()


def per_device(hidden_in, targets, norm_gain, up_weight, down_weight, start):
    vm, dma = pltpu.VMEM, pltpu.SemaphoreType.DMA
    any_spec = pl.BlockSpec(memory_space=pl.ANY)
    vmem_spec = pl.BlockSpec(memory_space=pltpu.VMEM)
    smem_spec = pl.BlockSpec(memory_space=pltpu.SMEM)
    scratch = [
        vm((HID, D), bf16),
        vm((HID, D), bf16),
        vm((ROWS, D), f32),
        vm((PAD, D), bf16),
        vm((TOK, D), bf16),
        vm((CHUNKS, N_Z, OWN, W), bf16),
        vm((BLK, D), f32),
        vm((GRP, D), f32),
        vm((3, CHUNKS, HALF, W), bf16),
        vm((3, CHUNKS, HALF, W), bf16),
        vm((2, HALF, D), f32),
        vm((3, CHUNKS, BLK, W), bf16),
        vm((3, CHUNKS, BLK, W), bf16),
        vm((3, CHUNKS, 2, BLK, W), bf16),
        vm((3, CHUNKS, 2, BLK, W), bf16),
        vm((3, CHUNKS, N_Z, OWN, W), bf16),
        vm((3, CHUNKS, N_Z - 1, OWN, W), bf16),
        vm((3, CHUNKS, N_Z, OWN, W), bf16),
        vm((3, GRP, D), bf16),
        vm((GRP, HID), f32),
        vm((GRP, HID), f32),
        vm((GRP, HID), bf16),
        vm((2, GRP, HID), f32),
        vm((GRP, HID), f32),
        vm((GRP, HID), f32),
        vm((TOK, PAD), f32),
        vm((N_X, GRP, PAD), f32),
        vm((TOK, HID), bf16),
        vm((2, N_X, GRP, PAD), bf16),
        vm((GRP, TOK), f32),
        vm((ROWS, D), f32),
        vm((ROWS, D), f32),
        vm((2, 3, 4, 8, 128), f32),
        vm((2, 2, 15, 4, 8, 128), f32),
        vm((3, OWN, D), f32),
        vm((OWN, D), f32),
        dma((2 * N_X + 1,)),
    ]
    pairs = [
        (CHUNKS, N_Z - 1), (CHUNKS, 4), (CHUNKS, 4),
        (4,), (4,), (4,), (12,), (4,),
        (3, CHUNKS), (3, CHUNKS, 2), (3, CHUNKS, 2), (3, CHUNKS, N_Z - 1),
        (3, CHUNKS, N_Z - 1), (3, CHUNKS, 4), (3, CHUNKS, 4),
        (N_X - 1,), (4,), (N_X - 1,), (2, 2, 15),
    ]
    for shape in pairs:
        scratch += [dma(shape), dma(shape)]
    scratch.append(dma((2,)))
    kw, k2, mix = pl.pallas_call(
        kernel,
        out_shape=(
            jax.ShapeDtypeStruct((ROWS, D), f32),
            jax.ShapeDtypeStruct((ROWS, D), f32),
            jax.ShapeDtypeStruct((9,), f32),
        ),
        in_specs=[vmem_spec, vmem_spec, vmem_spec, any_spec, any_spec, any_spec],
        out_specs=(any_spec, any_spec, smem_spec),
        scratch_shapes=scratch,
        compiler_params=pltpu.CompilerParams(
            collective_id=0, has_side_effects=True, vmem_limit_bytes=60 * 1024 * 1024
        ),
        cost_estimate=pl.CostEstimate(flops=5 * 10**9, bytes_accessed=14 * 10**6, transcendentals=10**5),
    )(hidden_in, targets, norm_gain, up_weight, down_weight, start)
    pieces = ROWS // PIECE
    return pl.pallas_call(
        combine,
        out_shape=(
            jax.ShapeDtypeStruct((2, ROWS, D), f32),
            jax.ShapeDtypeStruct((1,), f32),
            jax.ShapeDtypeStruct((2, 2), f32),
        ),
        in_specs=[smem_spec, any_spec, any_spec, any_spec],
        out_specs=(any_spec, smem_spec, smem_spec),
        scratch_shapes=[
            vm((ROWS, D), f32),
            vm((ROWS, D), f32),
            vm((ROWS, D), f32),
            vm((2, ROWS, D), f32),
            dma((3, pieces)),
            dma((2, pieces)),
        ],
        compiler_params=pltpu.CompilerParams(vmem_limit_bytes=60 * 1024 * 1024),
        cost_estimate=pl.CostEstimate(flops=10**7, bytes_accessed=9 * 10**6, transcendentals=0),
    )(mix, kw, k2, start)


def solution(mesh):
    placed = (
        P(("dp", "zero"), None),
        P(("dp", "zero"), None),
        P(),
        P("zero", None),
        P("zero", None),
        P(("zero", "dp"), None),
    )
    return jax.shard_map(
        per_device,
        mesh=mesh,
        in_specs=placed,
        out_specs=(P(None, ("zero", "dp"), None), P(), P()),
        check_vma=False,
    )
```

time: 1250 us -> 170 us (0.14)
  waiting for transfers between devices: 765 us -> 0 us
  blocking collectives: 382 us -> 0 us
  Pallas kernels: 0 us -> 170 us
  other arithmetic: 40.1 us -> 0 us
  matrix products: 33.6 us -> 0 us
  between operations: 18.9 us -> 0.8 us
  local copies, waits for them, and re-layouts: 13.2 us -> 0 us
    unnamed x12 -> x0, waiting for transfers between devices: 383 us -> none
    psum x5 -> x0, blocking collectives: 382 us -> none  [the longest x2 152 us: orthogonalize(): coeffs = lax.psum(local_coeffs, ('dp', 'zero')) / entry_count]
    all_gather x6 -> x0, waiting for transfers between devices: 299 us -> none  [the longest x3 226 us: spread_rows(): return lax.all_gather(local_rows, 'zero', axis=0, tiled=True)]
    pallas_call x0 -> x2, Pallas kernels: none -> 170 us  [the longest x1 164 us: per_device(): pl.pallas_call(kernel, out_shape=(jax.ShapeDtypeStruct((ROWS, D), f32), j...]
    reduce_scatter x2 -> x0, waiting for transfers between devices: 82.9 us -> none  [curvature(): lax.psum_scatter(contract_tokens(pre_grad_tangent, tokens).astype(jnp.bfl...]
    dot_general x9 -> x0, matrix products: 33.6 us -> none  [the longest x4 13.8 us: contract_hidden(): lax.dot_general(activations, weight, (((1,), (1,)), ((), ())), preferred_...]
    reduce_sum x9 -> x0, other arithmetic: 20.7 us -> none  [the longest x2 7.23 us: orthogonalize(): jnp.sum(leftover * leftover)]
    unnamed x23 -> x0, local copies, waits for them, and re-layouts: 12.6 us -> none
  transfers between devices with their start and end apart: 10 -> 0, of which waited for: 9 -> 0; matrix products, arithmetic and copies ran while one was open for 2% -> 0% of each run, Pallas kernels for 0% -> 0%
where the time goes in v1:
time: 170 us
  Pallas kernels  170 us (100%)
    pallas_call x1, Pallas kernels, per_device(): pl.pallas_call(kernel, out_shape=(jax.ShapeDtypeStruct((ROWS, D), f32), j...  164 us
    pallas_call x1, Pallas kernels, per_device(): pl.pallas_call(combine, out_shape=(jax.ShapeDtypeStruct((2, ROWS, D), f32...  5.71 us

profile of v1, /device:TPU:1, one launch (start us, length us, event | category | flops | bytes accessed | tf_op | source)
XLA Modules:
  0.0 170.3 jit_solution(16617575984307443582)
XLA Ops:
  0.6 163.8 %shard_map.85 = (f32[96,4608]{1,0:T(8,128)}, f32[96,4608]{1,0:T(8,128)}, f32[9]{0:T(128)}) custom-call(bf16[2,4608]{1,0:T(2,128)(2,1)} %hin.1, bf16[2,4608]{1,0:T(2,128)(2,1)} %tgt.1, f32[4608]{0:T(1024)} %gain.1, bf16[384,4608]{1,0:T(8,128)(2,1)} %up_hbm.1, bf16[384,4608]{1,0:T(8,128)(2,1)} %down_hbm.1, f32[96,4608]{1,0:T(8,128)} %start_hbm.3), custom_call_target="tpu_custom_call" | custom-call | flops 5000000000 | bytes 14000000 | tf_op jit(solution)/shard_map/pallas_call | solution.py:668
  164.5 5.7 %shard_map.86 = (f32[2,96,4608]{2,1,0:T(8,128)}, f32[1]{0:T(128)}, f32[2,2]{1,0:T(2,128)}) custom-call(f32[9]{0:T(128)} %get-tuple-element.6.mix, f32[96,4608]{1,0:T(8,128)} %get-tuple-element.7.kw_hbm, f32[96,4608]{1,0:T(8,128)} %get-tuple-element.8.k2_hbm, f32[96,4608]{1,0:T(8,128)} %start_hbm.3), custom_call_target="tpu_custom_call" | custom-call | flops 10000000 | bytes 9000000 | tf_op jit(solution)/shard_map/pallas_call | solution.py:684

commit v2 on v1

--- a/solution.py
+++ b/solution.py
@@ -22,7 +22,8 @@
 OWN = BLK // N_Z
 CHUNKS = 2
 W = D // CHUNKS
-PIECE = 16
+KEEP = 40
+PIECE = 32
 XA = 2560
 
 
@@ -117,7 +118,7 @@
     up, down, start, sbf, X, xz, tmp16, part,
     sb, rc, s1f, y1b, y1r, y2b, y2r, sz, rz, az, A,
     slope, bendag, hact, agrad, pt1, ptx, pts, ptr,
-    pfull, pr2, gram, kw, k2, arv, arr, tot, bsum,
+    pfull, pr2, g_hi, g_lo, kw, k2, arv, arr, tot, bsum,
     ld_sem, xz_s, xz_r, xy_s, xy_r, xc_s, xc_r,
     xa_s, xa_r, xac_s, xac_r, xb_s, xb_r, xby_s, xby_r, xbc_s, xbc_r,
     rc_s, rc_r, y1_s, y1_r, y2_s, y2_r, rz_s, rz_r,
@@ -131,6 +132,8 @@
     def dev(nx, ny, nz, nc):
         return (nx, ny * 16 + nz * 2 + nc)
 
+    pending = []
+
     def x_at(k):
         return (x + (k % N_X)) % N_X
 
@@ -159,14 +162,36 @@
             src_ref=src, dst_ref=dst, send_sem=ssem, recv_sem=rsem, device_id=to, device_id_type=MESH
         )
         cp.start()
+        pending.append(cp)
         return cp
+
+    def send_all(copies, bytes_of, ssem, rsem):
+        for src, dst, to in copies:
+            pltpu.make_async_remote_copy(
+                src_ref=src, dst_ref=dst, send_sem=ssem, recv_sem=rsem, device_id=to, device_id_type=MESH
+            ).start()
+        cp = pltpu.make_async_remote_copy(
+            src_ref=bytes_of,
+            dst_ref=bytes_of,
+            send_sem=ssem,
+            recv_sem=rsem,
+            device_id=c_peer,
+            device_id_type=MESH,
+        )
+        pending.append(cp)
+        return [cp]
+
+    def settle(keep=KEEP):
+        while len(pending) > keep:
+            pending.pop(0).wait_send()
 
     def rows(start_row, count):
         return pl.ds(pl.multiple_of(start_row, 16), count)
 
     def wait_all(cps):
+        settle()
         for cp in cps:
-            cp.wait()
+            cp.wait_recv()
 
     loads = []
     for b in range(N_X):
@@ -204,7 +229,7 @@
         second = []
         for b, (row_of, count) in enumerate(blocks):
             for j, to in enumerate((1, -1)):
-                first[b][j].wait()
+                wait_all([first[b][j]])
                 at = (rows(row_of(-to), count), pl.ds(c0 + j * half, half))
                 i = 2 * (nb + b) + j
                 second.append(send(ref.at[at], ref.at[at], ssem.at[i], rsem.at[i], peer(to)))
@@ -218,9 +243,8 @@
 
     def gather_z(own, buf, ssem, rsem):
         buf[z] = own
-        return [
-            send(buf.at[z], buf.at[z], ssem.at[k - 1], rsem.at[k - 1], z_peer(k)) for k in range(1, N_Z)
-        ]
+        copies = [(buf.at[z], buf.at[z], z_peer(k)) for k in range(1, N_Z)]
+        return send_all(copies, buf.at[pl.ds(0, N_Z - 1)], ssem, rsem)
 
     def join16(buf, c0, w):
         for j in range(N_Z):
@@ -304,16 +328,8 @@
         tmp16[:, cols] = block(0) + y2r[i, h, 0].astype(f32) + y2r[i, h, 1].astype(f32)
         for j in range(N_Z):
             sz[i, h, j] = tmp16[pl.ds(OWN * j, OWN), cols].astype(bf16)
-        cps = [
-            send(
-                sz.at[i, h, (z + k) % N_Z],
-                rz.at[i, h, k - 1],
-                rz_s.at[i, h, k - 1],
-                rz_r.at[i, h, k - 1],
-                z_peer(k),
-            )
-            for k in range(1, N_Z)
-        ]
+        copies = [(sz.at[i, h, (z + k) % N_Z], rz.at[i, h, k - 1], z_peer(k)) for k in range(1, N_Z)]
+        cps = send_all(copies, rz.at[i, h], rz_s.at[i, h], rz_r.at[i, h])
         yield
         wait_all(cps)
         s3 = sz[i, h, z].astype(f32)
@@ -329,16 +345,10 @@
 
     def all_sum(i, n):
         for s, peer in enumerate((xy_peer, zc_peer)):
-            cps = [
-                send(
-                    arv.at[i, s, pl.ds(0, n)],
-                    arr.at[i, s, k - 1, pl.ds(0, n)],
-                    ar_s.at[i, s, k - 1],
-                    ar_r.at[i, s, k - 1],
-                    peer(k),
-                )
-                for k in range(1, 16)
+            copies = [
+                (arv.at[i, s, pl.ds(0, n)], arr.at[i, s, k - 1, pl.ds(0, n)], peer(k)) for k in range(1, 16)
             ]
+            cps = send_all(copies, arr.at[i, s, :, pl.ds(0, n)], ar_s.at[i, s], ar_r.at[i, s])
             yield
             wait_all(cps)
             acc = arv[i, s, 0:n]
@@ -479,7 +489,10 @@
     def token_gram():
         half = TOK // 2
         for b in range(2):
-            gram[:, pl.ds(b * half, half)] = dot_t(X[group, :], X[pl.ds(b * half, half), :])
+            g = dot_t(X[group, :], X[pl.ds(b * half, half), :])
+            hi = g.astype(bf16)
+            g_hi[:, pl.ds(b * half, half)] = hi
+            g_lo[:, pl.ds(b * half, half)] = (g - hi.astype(f32)).astype(bf16)
             yield
 
     run(gathers(curv.astype(bf16), 1), token_gram())
@@ -487,7 +500,15 @@
     pfull[group, :] = p1.astype(bf16)
 
     def share_p1():
-        yield from ring_gather(pfull, [(lambda k: x_at(k) * GRP, GRP)], 0, HID, x_peer, pf_s, pf_r)
+        def use(k):
+            block = rows(x_at(k) * GRP, GRP)
+            term = dot(g_hi[:, block], pfull[block, :]) + dot(g_lo[:, block], pfull[block, :])
+            if k == 0:
+                ptx[...] = term
+            else:
+                ptx[...] = ptx[...] + term
+
+        yield from ring_gather(pfull, [(lambda k: x_at(k) * GRP, GRP)], 0, HID, x_peer, pf_s, pf_r, use)
 
     def own_sums():
         arv[0, 0, 0] = tile_sum(p1 * pt1[...])
@@ -495,10 +516,6 @@
 
     run(share_p1(), own_sums())
 
-    g = gram[...]
-    g_hi = g.astype(bf16)
-    g_lo = (g - g_hi.astype(f32)).astype(bf16)
-    ptx[...] = dot(g_hi, pfull[...]) + dot(g_lo, pfull[...])
     hact[...] = (slope[...] * ptx[...]).astype(bf16)
 
     def image_one():
@@ -539,14 +556,11 @@
         for k in range(1, N_X)
     ]
     wait_all(cps)
+    own = pr2[0].reshape(TOK, PAD).T
     sums = [None, None, None]
     for k in range(0, D, 512):
         cols = slice(k, k + 512)
-        acc = None
-        for b in range(N_X):
-            term = dot(pr2[0, b].T, X[pl.ds(b * GRP, GRP), cols])
-            acc = term if acc is None else acc + term
-        acc = acc[0:ROWS, :]
+        acc = dot(own, X[:, cols])[0:ROWS, :]
         k2[:, cols] = acc
         for j, other in enumerate((start[:, cols], kw[:, cols], acc)):
             s = tile_sum(other * acc)
@@ -577,6 +591,7 @@
         mix[j] = value[0, 0]
     out_w.wait()
     out_2.wait()
+    settle(0)
 
 
 def combine(mix, kw_hbm, k2_hbm, start_hbm, basis_hbm, quot, coef, kw, k2, start, out, in_sem, out_sem):
@@ -646,7 +661,8 @@
         vm((N_X, GRP, PAD), f32),
         vm((TOK, HID), bf16),
         vm((2, N_X, GRP, PAD), bf16),
-        vm((GRP, TOK), f32),
+        vm((GRP, TOK), bf16),
+        vm((GRP, TOK), bf16),
         vm((ROWS, D), f32),
         vm((ROWS, D), f32),
         vm((2, 3, 4, 8, 128), f32),
@@ -656,11 +672,11 @@
         dma((2 * N_X + 1,)),
     ]
     pairs = [
-        (CHUNKS, N_Z - 1), (CHUNKS, 4), (CHUNKS, 4),
+        (CHUNKS,), (CHUNKS, 4), (CHUNKS, 4),
         (4,), (4,), (4,), (12,), (4,),
-        (3, CHUNKS), (3, CHUNKS, 2), (3, CHUNKS, 2), (3, CHUNKS, N_Z - 1),
-        (3, CHUNKS, N_Z - 1), (3, CHUNKS, 4), (3, CHUNKS, 4),
-        (N_X - 1,), (4,), (N_X - 1,), (2, 2, 15),
+        (3, CHUNKS), (3, CHUNKS, 2), (3, CHUNKS, 2), (3, CHUNKS),
+        (3, CHUNKS), (3, CHUNKS, 4), (3, CHUNKS, 4),
+        (N_X - 1,), (4,), (N_X - 1,), (2, 2),
     ]
     for shape in pairs:
         scratch += [dma(shape), dma(shape)]

time: 170 us -> 165 us (0.971)
  Pallas kernels: 170 us -> 164 us
    pallas_call x1, Pallas kernels: 164 us -> 159 us  [per_device(): pl.pallas_call(kernel, out_shape=(jax.ShapeDtypeStruct((ROWS, D), f32), j...]
where the time goes in v2:
time: 165 us
  Pallas kernels  164 us (99%)
    pallas_call x1, Pallas kernels, per_device(): pl.pallas_call(kernel, out_shape=(jax.ShapeDtypeStruct((ROWS, D), f32), j...  159 us
    pallas_call x1, Pallas kernels, per_device(): pl.pallas_call(combine, out_shape=(jax.ShapeDtypeStruct((2, ROWS, D), f32...  5.05 us

profile of v2, /device:TPU:1, one launch (start us, length us, event | category | flops | bytes accessed | tf_op | source)
XLA Modules:
  0.0 165.1 jit_solution(3687044921724130618)
XLA Ops:
  0.6 159.2 %shard_map.85 = (f32[96,4608]{1,0:T(8,128)}, f32[96,4608]{1,0:T(8,128)}, f32[9]{0:T(128)}) custom-call(bf16[2,4608]{1,0:T(2,128)(2,1)} %hin.1, bf16[2,4608]{1,0:T(2,128)(2,1)} %tgt.1, f32[4608]{0:T(1024)} %gain.1, bf16[384,4608]{1,0:T(8,128)(2,1)} %up_hbm.1, bf16[384,4608]{1,0:T(8,128)(2,1)} %down_hbm.1, f32[96,4608]{1,0:T(8,128)} %start_hbm.3), custom_call_target="tpu_custom_call" | custom-call | flops 5000000000 | bytes 14000000 | tf_op jit(solution)/shard_map/pallas_call | solution.py:684
  159.8 5.0 %shard_map.86 = (f32[2,96,4608]{2,1,0:T(8,128)}, f32[1]{0:T(128)}, f32[2,2]{1,0:T(2,128)}) custom-call(f32[9]{0:T(128)} %get-tuple-element.6.mix, f32[96,4608]{1,0:T(8,128)} %get-tuple-element.7.kw_hbm, f32[96,4608]{1,0:T(8,128)} %get-tuple-element.8.k2_hbm, f32[96,4608]{1,0:T(8,128)} %start_hbm.3), custom_call_target="tpu_custom_call" | custom-call | flops 10000000 | bytes 9000000 | tf_op jit(solution)/shard_map/pallas_call | solution.py:700

commit v3 on v2

--- a/solution.py
+++ b/solution.py
@@ -117,8 +117,8 @@
     kw_hbm, k2_hbm, mix,
     up, down, start, sbf, X, xz, tmp16, part,
     sb, rc, s1f, y1b, y1r, y2b, y2r, sz, rz, az, A,
-    slope, bendag, hact, agrad, pt1, ptx, pts, ptr,
-    pfull, pr2, g_hi, g_lo, kw, k2, arv, arr, tot, bsum,
+    slope, bendag, hact, agrad, pt1, ptx, pts,
+    pfull, pr2, gram, kw, k2, arv, arr, tot, bsum,
     ld_sem, xz_s, xz_r, xy_s, xy_r, xc_s, xc_r,
     xa_s, xa_r, xac_s, xac_r, xb_s, xb_r, xby_s, xby_r, xbc_s, xbc_r,
     rc_s, rc_r, y1_s, y1_r, y2_s, y2_r, rz_s, rz_r,
@@ -211,7 +211,7 @@
         pl.semaphore_signal(barrier, inc=1, device_id=p, device_id_type=MESH)
     pl.semaphore_wait(barrier, len(peers))
 
-    def ring_gather(ref, blocks, c0, w, peer, ssem, rsem, then=None):
+    def ring_gather(ref, blocks, c0, w, peer, ssem, rsem, then=None, by_rows=False):
         half = w // 2
         nb = len(blocks)
         first = []
@@ -230,7 +230,10 @@
         for b, (row_of, count) in enumerate(blocks):
             for j, to in enumerate((1, -1)):
                 wait_all([first[b][j]])
-                at = (rows(row_of(-to), count), pl.ds(c0 + j * half, half))
+                if by_rows:
+                    at = (rows(row_of(-to) + j * (count // 2), count // 2), pl.ds(c0, w))
+                else:
+                    at = (rows(row_of(-to), count), pl.ds(c0 + j * half, half))
                 i = 2 * (nb + b) + j
                 second.append(send(ref.at[at], ref.at[at], ssem.at[i], rsem.at[i], peer(to)))
         if then:
@@ -276,7 +279,7 @@
         )
         yield
         wait_all(passed)
-        part_grad = dot_t(out[:, cols], down[:, cols])
+        part_grad = dot_t(down[:, cols], out[:, cols])
         if h == 0:
             agrad[i % 2] = part_grad
         else:
@@ -383,7 +386,7 @@
         )
         yield
         wait_all(passed)
-        pre = dot_t(X[group, cols], up[:, cols])
+        pre = dot_t(up[:, cols], X[group, cols])
         if h == 0:
             agrad[0] = pre
         else:
@@ -446,36 +449,41 @@
         for k in range(h * W, (h + 1) * W, W // 3):
             part[:, k : k + W // 3] = dot(hact[...], down[:, k : k + W // 3])
 
+    def to_act(b, tangent):
+        hid = pl.ds(b * PAD, PAD)
+        hact[:, hid] = (slope[hid, :] * tangent[hid, :]).T.astype(bf16)
+
     def weights():
         return tgt[...].astype(f32), gain[...]
 
     def forward():
         for b in range(N_X):
-            cols = pl.ds(b * PAD, PAD)
-            value, first, second = gelu_parts(agrad[0, :, cols])
-            hact[:, cols] = value.astype(bf16)
-            slope[:, cols] = first
-            bendag[:, cols] = second
+            hid = pl.ds(b * PAD, PAD)
+            value, first, second = gelu_parts(agrad[0, hid, :])
+            hact[:, hid] = value.T.astype(bf16)
+            slope[hid, :] = first
+            bendag[hid, :] = second
         yield from scatters(0, to_branch)
         bsum[...] = hin[...].astype(f32) + tot[0]
         yield from gathers(loss_grad(bsum[...], *weights()).astype(bf16), 0)
         bendag[...] = bendag[...] * agrad[0]
 
     def first_tangent():
-        pts[...] = dot_t(X[...], sbf[...])
-        ptr[x] = pts[group, :]
+        prod = dot_t(X[...], sbf[...])
+        for b in range(N_X):
+            pts[pl.ds(b * PAD, PAD), :] = prod[b * GRP : (b + 1) * GRP, :].T
+        own = rows(x * PAD, PAD)
+        pt1[own, :] = pts[own, :]
         cps = [
             send(
-                pts.at[rows(x_at(k) * GRP, GRP)], ptr.at[x], pt_s.at[k - 1], pt_r.at[k - 1], x_peer(k)
+                pts.at[rows(x_at(k) * PAD, PAD)], pt1.at[own], pt_s.at[k - 1], pt_r.at[k - 1], x_peer(k)
             )
             for k in range(1, N_X)
         ]
         yield
         wait_all(cps)
         for b in range(N_X):
-            cols = pl.ds(b * PAD, PAD)
-            pt1[:, cols] = ptr[b]
-            hact[:, cols] = (slope[:, cols] * ptr[b]).astype(bf16)
+            to_act(b, pt1)
         yield from scatters(1, to_branch)
 
     fwd = forward()
@@ -488,27 +496,29 @@
 
     def token_gram():
         half = TOK // 2
-        for b in range(2):
-            g = dot_t(X[group, :], X[pl.ds(b * half, half), :])
+        for b in range(0, TOK, half):
+            g = dot_t(X[pl.ds(b, half), :], X[group, :])
             hi = g.astype(bf16)
-            g_hi[:, pl.ds(b * half, half)] = hi
-            g_lo[:, pl.ds(b * half, half)] = (g - hi.astype(f32)).astype(bf16)
+            gram[pl.ds(b, half), pl.ds(0, GRP)] = hi
+            gram[pl.ds(b, half), pl.ds(GRP, GRP)] = (g - hi.astype(f32)).astype(bf16)
             yield
 
     run(gathers(curv.astype(bf16), 1), token_gram())
     p1 = agrad[1] * slope[...] + bendag[...] * pt1[...]
-    pfull[group, :] = p1.astype(bf16)
+    pfull[rows(x * HID, HID), :] = p1.astype(bf16)
 
     def share_p1():
         def use(k):
-            block = rows(x_at(k) * GRP, GRP)
-            term = dot(g_hi[:, block], pfull[block, :]) + dot(g_lo[:, block], pfull[block, :])
+            both_parts = dot(pfull[rows(x_at(k) * HID, HID), :], gram[rows(x_at(k) * GRP, GRP), :])
+            term = both_parts[:, 0:GRP] + both_parts[:, GRP : 2 * GRP]
             if k == 0:
                 ptx[...] = term
             else:
                 ptx[...] = ptx[...] + term
 
-        yield from ring_gather(pfull, [(lambda k: x_at(k) * GRP, GRP)], 0, HID, x_peer, pf_s, pf_r, use)
+        yield from ring_gather(
+            pfull, [(lambda k: x_at(k) * HID, HID)], 0, GRP, x_peer, pf_s, pf_r, use, by_rows=True
+        )
 
     def own_sums():
         arv[0, 0, 0] = tile_sum(p1 * pt1[...])
@@ -516,10 +526,11 @@
 
     run(share_p1(), own_sums())
 
-    hact[...] = (slope[...] * ptx[...]).astype(bf16)
+    for b in range(N_X):
+        to_act(b, ptx)
 
     def image_one():
-        own = pfull[:, pl.ds(pl.multiple_of(x * PAD, PAD), PAD)].T
+        own = jnp.concatenate([pfull[rows(b * HID + x * PAD, PAD), :] for b in range(N_X)], axis=1)
         for k in range(0, D, 512):
             kw[:, k : k + 512] = dot(own, X[:, k : k + 512])[0:ROWS, :]
             if k % 1536 == 1024:
@@ -548,15 +559,15 @@
     out_w = pltpu.make_async_copy(kw, kw_hbm, out_sem.at[0])
     out_w.start()
     for b in range(N_X):
-        cols = pl.ds(b * PAD, PAD)
-        pr2[1, b] = (agrad[0, :, cols] * slope[:, cols] + bendag[:, cols] * ptx[:, cols]).astype(bf16)
+        hid = pl.ds(b * PAD, PAD)
+        pr2[1, b] = (agrad[0, hid, :] * slope[hid, :] + bendag[hid, :] * ptx[hid, :]).astype(bf16)
     pr2[0, x] = pr2[1, x]
     cps = [
         send(pr2.at[1, x_at(k)], pr2.at[0, x], p2_s.at[k - 1], p2_r.at[k - 1], x_peer(k))
         for k in range(1, N_X)
     ]
     wait_all(cps)
-    own = pr2[0].reshape(TOK, PAD).T
+    own = jnp.concatenate([pr2[0, b] for b in range(N_X)], axis=1)
     sums = [None, None, None]
     for k in range(0, D, 512):
         cols = slice(k, k + 512)
@@ -651,18 +662,16 @@
         vm((3, CHUNKS, N_Z - 1, OWN, W), bf16),
         vm((3, CHUNKS, N_Z, OWN, W), bf16),
         vm((3, GRP, D), bf16),
-        vm((GRP, HID), f32),
-        vm((GRP, HID), f32),
+        vm((HID, GRP), f32),
+        vm((HID, GRP), f32),
         vm((GRP, HID), bf16),
-        vm((2, GRP, HID), f32),
-        vm((GRP, HID), f32),
-        vm((GRP, HID), f32),
-        vm((TOK, PAD), f32),
-        vm((N_X, GRP, PAD), f32),
-        vm((TOK, HID), bf16),
-        vm((2, N_X, GRP, PAD), bf16),
-        vm((GRP, TOK), bf16),
-        vm((GRP, TOK), bf16),
+        vm((2, HID, GRP), f32),
+        vm((HID, GRP), f32),
+        vm((HID, GRP), f32),
+        vm((HID, GRP), f32),
+        vm((N_X * HID, GRP), bf16),
+        vm((2, N_X, PAD, GRP), bf16),
+        vm((TOK, 2 * GRP), bf16),
         vm((ROWS, D), f32),
         vm((ROWS, D), f32),
         vm((2, 3, 4, 8, 128), f32),

time: 165 us -> 168 us (1.018)
  Pallas kernels: 164 us -> 167 us
    pallas_call x1, Pallas kernels: 159 us -> 162 us  [per_device(): pl.pallas_call(kernel, out_shape=(jax.ShapeDtypeStruct((ROWS, D), f32), j...]
where the time goes in v3:
time: 168 us; the launch traced here: 167 us
  Pallas kernels  167 us (99%)
    pallas_call x1, Pallas kernels, per_device(): pl.pallas_call(kernel, out_shape=(jax.ShapeDtypeStruct((ROWS, D), f32), j...  162 us
    pallas_call x1, Pallas kernels, per_device(): pl.pallas_call(combine, out_shape=(jax.ShapeDtypeStruct((2, ROWS, D), f32...  5.05 us

profile of v3, /device:TPU:1, one launch (start us, length us, event | category | flops | bytes accessed | tf_op | source)
XLA Modules:
  0.0 167.4 jit_solution(2711054760458261753)
XLA Ops:
  0.6 161.5 %shard_map.85 = (f32[96,4608]{1,0:T(8,128)}, f32[96,4608]{1,0:T(8,128)}, f32[9]{0:T(128)}) custom-call(bf16[2,4608]{1,0:T(2,128)(2,1)} %hin.1, bf16[2,4608]{1,0:T(2,128)(2,1)} %tgt.1, f32[4608]{0:T(1024)} %gain.1, bf16[384,4608]{1,0:T(8,128)(2,1)} %up_hbm.1, bf16[384,4608]{1,0:T(8,128)(2,1)} %down_hbm.1, f32[96,4608]{1,0:T(8,128)} %start_hbm.3), custom_call_target="tpu_custom_call" | custom-call | flops 5000000000 | bytes 14000000 | tf_op jit(solution)/shard_map/pallas_call | solution.py:693
  162.2 5.0 %shard_map.86 = (f32[2,96,4608]{2,1,0:T(8,128)}, f32[1]{0:T(128)}, f32[2,2]{1,0:T(2,128)}) custom-call(f32[9]{0:T(128)} %get-tuple-element.6.mix, f32[96,4608]{1,0:T(8,128)} %get-tuple-element.7.kw_hbm, f32[96,4608]{1,0:T(8,128)} %get-tuple-element.8.k2_hbm, f32[96,4608]{1,0:T(8,128)} %start_hbm.3), custom_call_target="tpu_custom_call" | custom-call | flops 10000000 | bytes 9000000 | tf_op jit(solution)/shard_map/pallas_call | solution.py:709

commit v4 on v2

--- a/solution.py
+++ b/solution.py
@@ -24,7 +24,6 @@
 W = D // CHUNKS
 KEEP = 40
 PIECE = 32
-XA = 2560
 
 
 def gelu_value(inputs):
@@ -115,15 +114,15 @@
 def kernel(
     hin, tgt, gain, up_hbm, down_hbm, start_hbm,
     kw_hbm, k2_hbm, mix,
-    up, down, start, sbf, X, xz, tmp16, part,
+    up, down, start, dirs, X, xz, tmp16, part,
     sb, rc, s1f, y1b, y1r, y2b, y2r, sz, rz, az, A,
-    slope, bendag, hact, agrad, pt1, ptx, pts, ptr,
+    slope, bendag, hact, agrad, pt1, ptx,
     pfull, pr2, g_hi, g_lo, kw, k2, arv, arr, tot, bsum,
     ld_sem, xz_s, xz_r, xy_s, xy_r, xc_s, xc_r,
-    xa_s, xa_r, xac_s, xac_r, xb_s, xb_r, xby_s, xby_r, xbc_s, xbc_r,
+    xa_s, xa_r, xac_s, xac_r, sx_s, sx_r,
     rc_s, rc_r, y1_s, y1_r, y2_s, y2_r, rz_s, rz_r,
     az_s, az_r, ay_s, ay_r, ac_s, ac_r,
-    pt_s, pt_r, pf_s, pf_r, p2_s, p2_r, ar_s, ar_r, out_sem,
+    pf_s, pf_r, p2_s, p2_r, ar_s, ar_r, out_sem,
 ):
     x = lax.axis_index("dp")
     shard = lax.axis_index("zero")
@@ -389,58 +388,64 @@
         else:
             agrad[0] = agrad[0] + pre
 
+    def accumulate_pt1(h, k):
+        cols = pl.ds(h * W, W)
+        block = rows(x_at(k) * PAD, PAD)
+        lanes = pl.ds(pl.multiple_of(x_at(k) * PAD, PAD), PAD)
+        term = dot_t(X[group, cols], dirs[block, cols])
+        if h == 0:
+            pt1[:, lanes] = term
+        else:
+            pt1[:, lanes] = pt1[:, lanes] + term
+
+    def start_rows(h):
+        ring = ring_gather(
+            dirs, [(lambda k: x_at(k) * PAD, ROWS)], h * W, W, x_peer, sx_s.at[h], sx_r.at[h]
+        )
+        next(ring)
+        yield
+        next(ring)
+        yield
+        for k in (0, -1, 1):
+            accumulate_pt1(h, k)
+        yield
+        run(ring)
+        accumulate_pt1(h, 2)
+
+    def other_tokens(h):
+        cols = pl.ds(h * W, W)
+        passed = []
+
+        def pass_on(k):
+            if k != 0:
+                at = (rows(x_at(k) * GRP + c * HALF, HALF), cols)
+                passed.append(send(X.at[at], X.at[at], xac_s.at[h, k % 4], xac_r.at[h, k % 4], c_peer))
+
+        yield from ring_gather(
+            X, [(lambda k: x_at(k) * GRP + c * HALF, HALF)], h * W, W, x_peer, xa_s.at[h], xa_r.at[h], pass_on
+        )
+        yield
+        wait_all(passed)
+
     def local_work():
+        loads[-1].wait()
+        dirs[rows(x * PAD, ROWS), :] = start[...].astype(bf16)
+        for g in s_gens:
+            next(g)
         for b in range(N_X):
-            up[pl.ds(b * PAD + ROWS, PAD - ROWS), :] = jnp.zeros((PAD - ROWS, D), bf16)
-            down[pl.ds(b * PAD + ROWS, PAD - ROWS), :] = jnp.zeros((PAD - ROWS, D), bf16)
-        sbf[pl.ds(ROWS, PAD - ROWS), :] = jnp.zeros((PAD - ROWS, D), bf16)
-        yield
-        for cp in loads:
+            pad = pl.ds(b * PAD + ROWS, PAD - ROWS)
+            up[pad, :] = jnp.zeros((PAD - ROWS, D), bf16)
+            down[pad, :] = jnp.zeros((PAD - ROWS, D), bf16)
+            dirs[pad, :] = jnp.zeros((PAD - ROWS, D), bf16)
+        yield
+        for cp in loads[:-1]:
             cp.wait()
-        sbf[pl.ds(0, ROWS), :] = start[...].astype(bf16)
-        yield
         arv[0, 0, 1] = tile_sum(start[...] * start[...])
 
-    own_xb = ring_gather(
-        X, [(lambda k: x_at(k) * GRP + c * HALF + y * BLK, BLK)], XA, D - XA, x_peer, xb_s, xb_r
-    )
-    tok_gens = [group_tokens(h) for h in range(CHUNKS)]
-
-    def later_xb():
-        for _ in range(2):
-            next(own_xb)
-            yield
-
+    s_gens = [start_rows(h) for h in range(CHUNKS)]
     both = list(range(CHUNKS))
     n = CHUNKS
-    play(tok_gens + [local_work(), later_xb()], both + [n] + both + [n + 1, n] + both + [n + 1, n] + both)
-
-    def tokens_yx():
-        passed = []
-
-        def pass_on(k):
-            if k != 0:
-                at = (rows(x_at(k) * GRP + c * HALF, HALF), pl.ds(0, XA))
-                passed.append(send(X.at[at], X.at[at], xac_s.at[k % 4], xac_r.at[k % 4], c_peer))
-
-        yield from ring_gather(
-            X, [(lambda k: x_at(k) * GRP + c * HALF, HALF)], 0, XA, x_peer, xa_s, xa_r, pass_on
-        )
-        yield
-        wait_all(passed)
-
-    def tokens_xy():
-        next(own_xb, None)
-        blocks = [
-            (lambda k, b=b: x_at(b) * GRP + c * HALF + y_at(k) * BLK, BLK) for b in range(1, N_X)
-        ]
-        yield from ring_gather(X, blocks, XA, D - XA, y_peer, xby_s, xby_r)
-        passed = []
-        for b in range(1, N_X):
-            at = (rows(x_at(b) * GRP + c * HALF, HALF), pl.ds(XA, D - XA))
-            passed.append(send(X.at[at], X.at[at], xbc_s.at[b], xbc_r.at[b], c_peer))
-        yield
-        wait_all(passed)
+    play([group_tokens(h) for h in range(CHUNKS)] + [local_work()], both + [n] + both + [n] + both + both)
 
     def to_branch(h):
         for k in range(h * W, (h + 1) * W, W // 3):
@@ -462,28 +467,17 @@
         bendag[...] = bendag[...] * agrad[0]
 
     def first_tangent():
-        pts[...] = dot_t(X[...], sbf[...])
-        ptr[x] = pts[group, :]
-        cps = [
-            send(
-                pts.at[rows(x_at(k) * GRP, GRP)], ptr.at[x], pt_s.at[k - 1], pt_r.at[k - 1], x_peer(k)
-            )
-            for k in range(1, N_X)
-        ]
-        yield
-        wait_all(cps)
-        for b in range(N_X):
-            cols = pl.ds(b * PAD, PAD)
-            pt1[:, cols] = ptr[b]
-            hact[:, cols] = (slope[:, cols] * ptr[b]).astype(bf16)
+        hact[...] = (slope[...] * pt1[...]).astype(bf16)
         yield from scatters(1, to_branch)
 
     fwd = forward()
-    yx, xy = tokens_yx(), tokens_xy()
-    for g in (yx, xy, fwd, xy, fwd, xy, fwd, yx, fwd, yx, fwd, xy, yx):
+    others = [other_tokens(h) for h in range(CHUNKS)]
+    for g in s_gens + [fwd] + s_gens + [fwd, fwd] + s_gens:
         next(g, None)
-    run(xy, yx)
-    play((first_tangent(), fwd), (0, 1, 0, 1))
+    tangent = first_tangent()
+    for g in [tangent, fwd] + others:
+        next(g, None)
+    run(tangent, fwd)
     curv = loss_curv(bsum[...], tot[1], *weights())
 
     def token_gram():
@@ -495,7 +489,11 @@
             g_lo[:, pl.ds(b * half, half)] = (g - hi.astype(f32)).astype(bf16)
             yield
 
-    run(gathers(curv.astype(bf16), 1), token_gram())
+    grads = gathers(curv.astype(bf16), 1)
+    for g in [grads] + others + [grads] + others + [grads] + others + [grads]:
+        next(g, None)
+    run(token_gram())
+    run(grads)
     p1 = agrad[1] * slope[...] + bendag[...] * pt1[...]
     pfull[group, :] = p1.astype(bf16)
 
@@ -508,7 +506,15 @@
             else:
                 ptx[...] = ptx[...] + term
 
-        yield from ring_gather(pfull, [(lambda k: x_at(k) * GRP, GRP)], 0, HID, x_peer, pf_s, pf_r, use)
+        cps = [
+            send(pfull.at[group], pfull.at[group], pf_s.at[k - 1], pf_r.at[k - 1], x_peer(k))
+            for k in range(1, N_X)
+        ]
+        use(0)
+        yield
+        for k in (1, 3, 2):
+            wait_all([cps[k - 1]])
+            use(N_X - k)
 
     def own_sums():
         arv[0, 0, 0] = tile_sum(p1 * pt1[...])
@@ -635,7 +641,7 @@
         vm((HID, D), bf16),
         vm((HID, D), bf16),
         vm((ROWS, D), f32),
-        vm((PAD, D), bf16),
+        vm((HID, D), bf16),
         vm((TOK, D), bf16),
         vm((CHUNKS, N_Z, OWN, W), bf16),
         vm((BLK, D), f32),
@@ -657,8 +663,6 @@
         vm((2, GRP, HID), f32),
         vm((GRP, HID), f32),
         vm((GRP, HID), f32),
-        vm((TOK, PAD), f32),
-        vm((N_X, GRP, PAD), f32),
         vm((TOK, HID), bf16),
         vm((2, N_X, GRP, PAD), bf16),
         vm((GRP, TOK), bf16),
@@ -673,10 +677,10 @@
     ]
     pairs = [
         (CHUNKS,), (CHUNKS, 4), (CHUNKS, 4),
-        (4,), (4,), (4,), (12,), (4,),
+        (CHUNKS, 4), (CHUNKS, 4), (CHUNKS, 4),
         (3, CHUNKS), (3, CHUNKS, 2), (3, CHUNKS, 2), (3, CHUNKS),
         (3, CHUNKS), (3, CHUNKS, 4), (3, CHUNKS, 4),
-        (N_X - 1,), (4,), (N_X - 1,), (2, 2),
+        (N_X - 1,), (N_X - 1,), (2, 2),
     ]
     for shape in pairs:
         scratch += [dma(shape), dma(shape)]

time: 165 us -> 157 us (0.952)
  Pallas kernels: 164 us -> 156 us
    pallas_call x1, Pallas kernels: 159 us -> 151 us  [per_device(): pl.pallas_call(kernel, out_shape=(jax.ShapeDtypeStruct((ROWS, D), f32), j...]
where the time goes in v4:
time: 157 us; the launch traced here: 156 us
  Pallas kernels  156 us (99%)
    pallas_call x1, Pallas kernels, per_device(): pl.pallas_call(kernel, out_shape=(jax.ShapeDtypeStruct((ROWS, D), f32), j...  151 us
    pallas_call x1, Pallas kernels, per_device(): pl.pallas_call(combine, out_shape=(jax.ShapeDtypeStruct((2, ROWS, D), f32...  5.05 us

profile of v4, /device:TPU:1, one launch (start us, length us, event | category | flops | bytes accessed | tf_op | source)
XLA Modules:
  0.0 156.4 jit_solution(1905211508308086850)
XLA Ops:
  0.6 150.6 %shard_map.85 = (f32[96,4608]{1,0:T(8,128)}, f32[96,4608]{1,0:T(8,128)}, f32[9]{0:T(128)}) custom-call(bf16[2,4608]{1,0:T(2,128)(2,1)} %hin.1, bf16[2,4608]{1,0:T(2,128)(2,1)} %tgt.1, f32[4608]{0:T(1024)} %gain.1, bf16[384,4608]{1,0:T(8,128)(2,1)} %up_hbm.1, bf16[384,4608]{1,0:T(8,128)(2,1)} %down_hbm.1, f32[96,4608]{1,0:T(8,128)} %start_hbm.3), custom_call_target="tpu_custom_call" | custom-call | flops 5000000000 | bytes 14000000 | tf_op jit(solution)/shard_map/pallas_call | solution.py:688
  151.2 5.0 %shard_map.86 = (f32[2,96,4608]{2,1,0:T(8,128)}, f32[1]{0:T(128)}, f32[2,2]{1,0:T(2,128)}) custom-call(f32[9]{0:T(128)} %get-tuple-element.6.mix, f32[96,4608]{1,0:T(8,128)} %get-tuple-element.7.kw_hbm, f32[96,4608]{1,0:T(8,128)} %get-tuple-element.8.k2_hbm, f32[96,4608]{1,0:T(8,128)} %start_hbm.3), custom_call_target="tpu_custom_call" | custom-call | flops 10000000 | bytes 9000000 | tf_op jit(solution)/shard_map/pallas_call | solution.py:704

commit v5 on v4

--- a/solution.py
+++ b/solution.py
@@ -115,7 +115,7 @@
     hin, tgt, gain, up_hbm, down_hbm, start_hbm,
     kw_hbm, k2_hbm, mix,
     up, down, start, dirs, X, xz, tmp16, part,
-    sb, rc, s1f, y1b, y1r, y2b, y2r, sz, rz, az, A,
+    sb, rc, y1b, y1r, y2b, y2r, sz, rz, az, A,
     slope, bendag, hact, agrad, pt1, ptx,
     pfull, pr2, g_hi, g_lo, kw, k2, arv, arr, tot, bsum,
     ld_sem, xz_s, xz_r, xy_s, xy_r, xc_s, xc_r,
@@ -149,6 +149,9 @@
         return dev(x, y, (z + k) % N_Z, c)
 
     c_peer = dev(x, y, z, 1 - c)
+
+    def cross_peer(k):
+        return dev(x, y_at(k), z, 1 - c)
 
     def xy_peer(k):
         return dev(x_at(k // N_Y), y_at(k % N_Y), z, c)
@@ -206,11 +209,12 @@
 
     barrier = pltpu.get_barrier_semaphore()
     peers = [xy_peer(k) for k in range(1, N_X * N_Y)] + [zc_peer(k) for k in range(1, N_Z * N_C)]
+    peers += [cross_peer(1), cross_peer(-1)]
     for p in peers:
         pl.semaphore_signal(barrier, inc=1, device_id=p, device_id_type=MESH)
     pl.semaphore_wait(barrier, len(peers))
 
-    def ring_gather(ref, blocks, c0, w, peer, ssem, rsem, then=None):
+    def ring_gather(ref, blocks, c0, w, peer, ssem, rsem, then=None, cross=None):
         half = w // 2
         nb = len(blocks)
         first = []
@@ -232,6 +236,8 @@
                 at = (rows(row_of(-to), count), pl.ds(c0 + j * half, half))
                 i = 2 * (nb + b) + j
                 second.append(send(ref.at[at], ref.at[at], ssem.at[i], rsem.at[i], peer(to)))
+                if cross:
+                    second.append(send(ref.at[at], ref.at[at], ssem.at[i + 2], rsem.at[i + 2], cross(to)))
         if then:
             then(-1)
             then(1)
@@ -260,8 +266,9 @@
         passed = []
 
         def pass_on(k):
-            at = (rows(c * HALF + y_at(k) * BLK, BLK), cols)
-            passed.append(send(out.at[at], out.at[at], ac_s.at[i, h, k % 4], ac_r.at[i, h, k % 4], c_peer))
+            if k != 2:
+                at = (rows(c * HALF + y_at(k) * BLK, BLK), cols)
+                passed.append(send(out.at[at], out.at[at], ac_s.at[i, h, k % 4], ac_r.at[i, h, k % 4], c_peer))
 
         yield from ring_gather(
             out,
@@ -272,8 +279,8 @@
             ay_s.at[i, h],
             ay_r.at[i, h],
             pass_on,
+            cross_peer,
         )
-        yield
         wait_all(passed)
         part_grad = dot_t(out[:, cols], down[:, cols])
         if h == 0:
@@ -281,50 +288,53 @@
         else:
             agrad[i % 2] = agrad[i % 2] + part_grad
 
-    def scatter(i, h, make=None):
+    def scatter(i, h, make):
         c0 = h * W
         cols = slice(c0, c0 + W)
-        if make is not None:
-            make(h)
-        sb[i, h] = part[rows((1 - c) * HALF, HALF), cols].astype(bf16)
-        cps = [send(sb.at[i, h], rc.at[i, h], rc_s.at[i, h], rc_r.at[i, h], c_peer)]
-        yield
-        wait_all(cps)
-        s1f[i % 2, :, cols] = part[rows(c * HALF, HALF), cols] + rc[i, h].astype(f32)
-
-        def block(k):
-            return s1f[i % 2, rows(y_at(k) * BLK, BLK), cols]
+        make(i, h)
+        buf = part.at[i % 2]
+
+        def mine(k):
+            return buf[rows(c * HALF + y_at(k) * BLK, BLK), cols]
+
+        def other(k):
+            return buf[rows((1 - c) * HALF + y_at(k) * BLK, BLK), cols]
 
         half = W // 2
-        y1b[i, h] = block(2).astype(bf16)
+        y1b[i, h, 0] = mine(2).astype(bf16)
+        y1b[i, h, 1] = other(2).astype(bf16)
         cps = [
             send(
-                y1b.at[i, h, :, pl.ds(j * half, half)],
-                y1r.at[i, h, :, pl.ds(j * half, half)],
-                y1_s.at[i, h, j],
-                y1_r.at[i, h, j],
-                y_peer(to),
+                y1b.at[i, h, p, :, pl.ds(j * half, half)],
+                y1r.at[i, h, p, :, pl.ds(j * half, half)],
+                y1_s.at[i, h, 2 * p + j],
+                y1_r.at[i, h, 2 * p + j],
+                peer(to),
             )
+            for p, peer in enumerate((y_peer, cross_peer))
             for j, to in enumerate((1, -1))
         ]
+        for n, k in enumerate((0, 1, -1)):
+            sb[i, h, n] = other(k).astype(bf16)
+        cps.append(send(sb.at[i, h], rc.at[i, h], rc_s.at[i, h], rc_r.at[i, h], c_peer))
         yield
         wait_all(cps)
-        got = y1r[i, h].astype(f32)
+        got = y1r[i, h, 0].astype(f32) + y1r[i, h, 1].astype(f32)
         for j, to in enumerate((1, -1)):
-            mine = block(to)
-            if j == 0:
-                pieces = [mine[:, :half] + got[:, :half], mine[:, half:]]
-            else:
-                pieces = [mine[:, :half], mine[:, half:] + got[:, half:]]
-            y2b[i, h, j, :, pl.ds(0, half)] = pieces[0].astype(bf16)
-            y2b[i, h, j, :, pl.ds(half, half)] = pieces[1].astype(bf16)
+            both_cores = mine(to) + rc[i, h, 1 + j].astype(f32)
+            for p in range(2):
+                at = slice(p * half, (p + 1) * half)
+                piece = both_cores[:, at] + got[:, at] if p == j else both_cores[:, at]
+                y2b[i, h, j, :, at] = piece.astype(bf16)
         cps = [
             send(y2b.at[i, h, j], y2r.at[i, h, j], y2_s.at[i, h, j], y2_r.at[i, h, j], y_peer(to))
             for j, to in enumerate((1, -1))
         ]
         yield
         wait_all(cps)
-        tmp16[:, cols] = block(0) + y2r[i, h, 0].astype(f32) + y2r[i, h, 1].astype(f32)
+        tmp16[:, cols] = (
+            mine(0) + rc[i, h, 0].astype(f32) + y2r[i, h, 0].astype(f32) + y2r[i, h, 1].astype(f32)
+        )
         for j in range(N_Z):
             sz[i, h, j] = tmp16[pl.ds(OWN * j, OWN), cols].astype(bf16)
         copies = [(sz.at[i, h, (z + k) % N_Z], rz.at[i, h, k - 1], z_peer(k)) for k in range(1, N_Z)]
@@ -367,8 +377,9 @@
         passed = []
 
         def pass_on(k):
-            at = (rows(x * GRP + c * HALF + y_at(k) * BLK, BLK), cols)
-            passed.append(send(X.at[at], X.at[at], xc_s.at[h, k % 4], xc_r.at[h, k % 4], c_peer))
+            if k != 2:
+                at = (rows(x * GRP + c * HALF + y_at(k) * BLK, BLK), cols)
+                passed.append(send(X.at[at], X.at[at], xc_s.at[h, k % 4], xc_r.at[h, k % 4], c_peer))
 
         yield from ring_gather(
             X,
@@ -379,8 +390,8 @@
             xy_s.at[h],
             xy_r.at[h],
             pass_on,
+            cross_peer,
         )
-        yield
         wait_all(passed)
         pre = dot_t(X[group, cols], up[:, cols])
         if h == 0:
@@ -447,9 +458,9 @@
     n = CHUNKS
     play([group_tokens(h) for h in range(CHUNKS)] + [local_work()], both + [n] + both + [n] + both + both)
 
-    def to_branch(h):
+    def to_branch(i, h):
         for k in range(h * W, (h + 1) * W, W // 3):
-            part[:, k : k + W // 3] = dot(hact[...], down[:, k : k + W // 3])
+            part[i % 2, :, k : k + W // 3] = dot(hact[...], down[:, k : k + W // 3])
 
     def weights():
         return tgt[...].astype(f32), gain[...]
@@ -472,7 +483,7 @@
 
     fwd = forward()
     others = [other_tokens(h) for h in range(CHUNKS)]
-    for g in s_gens + [fwd] + s_gens + [fwd, fwd] + s_gens:
+    for g in s_gens + [fwd] + s_gens + [fwd] + s_gens + [fwd]:
         next(g, None)
     tangent = first_tangent()
     for g in [tangent, fwd] + others:
@@ -645,12 +656,11 @@
         vm((TOK, D), bf16),
         vm((CHUNKS, N_Z, OWN, W), bf16),
         vm((BLK, D), f32),
-        vm((GRP, D), f32),
-        vm((3, CHUNKS, HALF, W), bf16),
-        vm((3, CHUNKS, HALF, W), bf16),
-        vm((2, HALF, D), f32),
-        vm((3, CHUNKS, BLK, W), bf16),
-        vm((3, CHUNKS, BLK, W), bf16),
+        vm((2, GRP, D), f32),
+        vm((3, CHUNKS, 3, BLK, W), bf16),
+        vm((3, CHUNKS, 3, BLK, W), bf16),
+        vm((3, CHUNKS, 2, BLK, W), bf16),
+        vm((3, CHUNKS, 2, BLK, W), bf16),
         vm((3, CHUNKS, 2, BLK, W), bf16),
         vm((3, CHUNKS, 2, BLK, W), bf16),
         vm((3, CHUNKS, N_Z, OWN, W), bf16),
@@ -676,10 +686,10 @@
         dma((2 * N_X + 1,)),
     ]
     pairs = [
-        (CHUNKS,), (CHUNKS, 4), (CHUNKS, 4),
+        (CHUNKS,), (CHUNKS, 6), (CHUNKS, 4),
         (CHUNKS, 4), (CHUNKS, 4), (CHUNKS, 4),
-        (3, CHUNKS), (3, CHUNKS, 2), (3, CHUNKS, 2), (3, CHUNKS),
-        (3, CHUNKS), (3, CHUNKS, 4), (3, CHUNKS, 4),
+        (3, CHUNKS), (3, CHUNKS, 4), (3, CHUNKS, 2), (3, CHUNKS),
+        (3, CHUNKS), (3, CHUNKS, 6), (3, CHUNKS, 4),
         (N_X - 1,), (N_X - 1,), (2, 2),
     ]
     for shape in pairs:

time: 157 us -> 154 us (0.981)
  Pallas kernels: 156 us -> 153 us
    pallas_call x1, Pallas kernels: 151 us -> 148 us  [per_device(): pl.pallas_call(kernel, out_shape=(jax.ShapeDtypeStruct((ROWS, D), f32), j...]
where the time goes in v5:
time: 154 us
  Pallas kernels  153 us (99%)
    pallas_call x1, Pallas kernels, per_device(): pl.pallas_call(kernel, out_shape=(jax.ShapeDtypeStruct((ROWS, D), f32), j...  148 us
    pallas_call x1, Pallas kernels, per_device(): pl.pallas_call(combine, out_shape=(jax.ShapeDtypeStruct((2, ROWS, D), f32...  5.05 us

profile of v5, /device:TPU:1, one launch (start us, length us, event | category | flops | bytes accessed | tf_op | source)
XLA Modules:
  0.0 154.1 jit_solution(6246437792611840933)
XLA Ops:
  0.6 148.2 %shard_map.85 = (f32[96,4608]{1,0:T(8,128)}, f32[96,4608]{1,0:T(8,128)}, f32[9]{0:T(128)}) custom-call(bf16[2,4608]{1,0:T(2,128)(2,1)} %hin.1, bf16[2,4608]{1,0:T(2,128)(2,1)} %tgt.1, f32[4608]{0:T(1024)} %gain.1, bf16[384,4608]{1,0:T(8,128)(2,1)} %up_hbm.1, bf16[384,4608]{1,0:T(8,128)(2,1)} %down_hbm.1, f32[96,4608]{1,0:T(8,128)} %start_hbm.3), custom_call_target="tpu_custom_call" | custom-call | flops 5000000000 | bytes 14000000 | tf_op jit(solution)/shard_map/pallas_call | solution.py:698
  148.9 5.0 %shard_map.86 = (f32[2,96,4608]{2,1,0:T(8,128)}, f32[1]{0:T(128)}, f32[2,2]{1,0:T(2,128)}) custom-call(f32[9]{0:T(128)} %get-tuple-element.6.mix, f32[96,4608]{1,0:T(8,128)} %get-tuple-element.7.kw_hbm, f32[96,4608]{1,0:T(8,128)} %get-tuple-element.8.k2_hbm, f32[96,4608]{1,0:T(8,128)} %start_hbm.3), custom_call_target="tpu_custom_call" | custom-call | flops 10000000 | bytes 9000000 | tf_op jit(solution)/shard_map/pallas_call | solution.py:714

commit v6 on v5

--- a/solution.py
+++ b/solution.py
@@ -112,9 +112,9 @@
 
 
 def kernel(
-    hin, tgt, gain, up_hbm, down_hbm, start_hbm,
+    hin_hbm, tgt_hbm, gain_hbm, up_hbm, down_hbm, start_hbm,
     kw_hbm, k2_hbm, mix,
-    up, down, start, dirs, X, xz, tmp16, part,
+    hin, tgt, gain, up, down, start, dirs, X, xz, part,
     sb, rc, y1b, y1r, y2b, y2r, sz, rz, az, A,
     slope, bendag, hact, agrad, pt1, ptx,
     pfull, pr2, g_hi, g_lo, kw, k2, arv, arr, tot, bsum,
@@ -133,11 +133,15 @@
 
     pending = []
 
+    xs = [x] + [(x + k) % N_X for k in range(1, N_X)]
+    ys = [y] + [(y + k) % N_Y for k in range(1, N_Y)]
+    zs = [z] + [(z + k) % N_Z for k in range(1, N_Z)]
+
     def x_at(k):
-        return (x + (k % N_X)) % N_X
+        return xs[k % N_X]
 
     def y_at(k):
-        return (y + (k % N_Y)) % N_Y
+        return ys[k % N_Y]
 
     def x_peer(k):
         return dev(x_at(k), y, z, c)
@@ -146,7 +150,7 @@
         return dev(x, y_at(k), z, c)
 
     def z_peer(k):
-        return dev(x, y, (z + k) % N_Z, c)
+        return dev(x, y, zs[k], c)
 
     c_peer = dev(x, y, z, 1 - c)
 
@@ -157,7 +161,7 @@
         return dev(x_at(k // N_Y), y_at(k % N_Y), z, c)
 
     def zc_peer(k):
-        return dev(x, y, (z + k // N_C) % N_Z, (c + k % N_C) % N_C)
+        return dev(x, y, zs[k // N_C], c if k % N_C == 0 else 1 - c)
 
     def send(src, dst, ssem, rsem, to):
         cp = pltpu.make_async_remote_copy(
@@ -195,6 +199,12 @@
         for cp in cps:
             cp.wait_recv()
 
+    small = [
+        pltpu.make_async_copy(src, dst, ld_sem.at[2 * N_X + 1 + j])
+        for j, (src, dst) in enumerate(((hin_hbm, hin), (tgt_hbm, tgt), (gain_hbm, gain)))
+    ]
+    for cp in small:
+        cp.start()
     loads = []
     for b in range(N_X):
         for j, (src, dst) in enumerate(((up_hbm, up), (down_hbm, down))):
@@ -213,6 +223,8 @@
     for p in peers:
         pl.semaphore_signal(barrier, inc=1, device_id=p, device_id_type=MESH)
     pl.semaphore_wait(barrier, len(peers))
+    for cp in small:
+        cp.wait()
 
     def ring_gather(ref, blocks, c0, w, peer, ssem, rsem, then=None, cross=None):
         half = w // 2
@@ -251,10 +263,8 @@
         copies = [(buf.at[z], buf.at[z], z_peer(k)) for k in range(1, N_Z)]
         return send_all(copies, buf.at[pl.ds(0, N_Z - 1)], ssem, rsem)
 
-    def join16(buf, c0, w):
-        for j in range(N_Z):
-            tmp16[pl.ds(OWN * j, OWN), c0 : c0 + w] = buf[j].astype(f32)
-        return tmp16[:, c0 : c0 + w].astype(bf16)
+    def join16(buf):
+        return buf[...].reshape(BLK, W)
 
     def gather(own, i, h):
         c0, out = h * W, A.at[i]
@@ -262,7 +272,7 @@
         cps = gather_z(own[:, c0 : c0 + W], az.at[i, h], az_s.at[i, h], az_r.at[i, h])
         yield
         wait_all(cps)
-        out[rows(c * HALF + y * BLK, BLK), cols] = join16(az.at[i, h], c0, W)
+        out[rows(c * HALF + y * BLK, BLK), cols] = join16(az.at[i, h])
         passed = []
 
         def pass_on(k):
@@ -332,12 +342,9 @@
         ]
         yield
         wait_all(cps)
-        tmp16[:, cols] = (
-            mine(0) + rc[i, h, 0].astype(f32) + y2r[i, h, 0].astype(f32) + y2r[i, h, 1].astype(f32)
-        )
-        for j in range(N_Z):
-            sz[i, h, j] = tmp16[pl.ds(OWN * j, OWN), cols].astype(bf16)
-        copies = [(sz.at[i, h, (z + k) % N_Z], rz.at[i, h, k - 1], z_peer(k)) for k in range(1, N_Z)]
+        total = mine(0) + rc[i, h, 0].astype(f32) + y2r[i, h, 0].astype(f32) + y2r[i, h, 1].astype(f32)
+        sz[i, h] = total.astype(bf16).reshape(N_Z, OWN, W)
+        copies = [(sz.at[i, h, zs[k]], rz.at[i, h, k - 1], z_peer(k)) for k in range(1, N_Z)]
         cps = send_all(copies, rz.at[i, h], rz_s.at[i, h], rz_r.at[i, h])
         yield
         wait_all(cps)
@@ -373,7 +380,7 @@
         cps = gather_z(hin[:, c0 : c0 + W], xz.at[h], xz_s.at[h], xz_r.at[h])
         yield
         wait_all(cps)
-        X[rows(x * GRP + c * HALF + y * BLK, BLK), cols] = join16(xz.at[h], c0, W)
+        X[rows(x * GRP + c * HALF + y * BLK, BLK), cols] = join16(xz.at[h])
         passed = []
 
         def pass_on(k):
@@ -491,19 +498,17 @@
     run(tangent, fwd)
     curv = loss_curv(bsum[...], tot[1], *weights())
 
-    def token_gram():
-        half = TOK // 2
-        for b in range(2):
-            g = dot_t(X[group, :], X[pl.ds(b * half, half), :])
-            hi = g.astype(bf16)
-            g_hi[:, pl.ds(b * half, half)] = hi
-            g_lo[:, pl.ds(b * half, half)] = (g - hi.astype(f32)).astype(bf16)
-            yield
+    def token_gram(k):
+        mine = rows(x_at(k) * GRP, GRP)
+        g = dot_t(X[mine, :], X[...])
+        hi = g.astype(bf16)
+        g_hi[mine, :] = hi
+        g_lo[mine, :] = (g - hi.astype(f32)).astype(bf16)
 
     grads = gathers(curv.astype(bf16), 1)
     for g in [grads] + others + [grads] + others + [grads] + others + [grads]:
         next(g, None)
-    run(token_gram())
+    token_gram(0)
     run(grads)
     p1 = agrad[1] * slope[...] + bendag[...] * pt1[...]
     pfull[group, :] = p1.astype(bf16)
@@ -511,7 +516,7 @@
     def share_p1():
         def use(k):
             block = rows(x_at(k) * GRP, GRP)
-            term = dot(g_hi[:, block], pfull[block, :]) + dot(g_lo[:, block], pfull[block, :])
+            term = dot(g_hi[group, block], pfull[block, :]) + dot(g_lo[group, block], pfull[block, :])
             if k == 0:
                 ptx[...] = term
             else:
@@ -558,6 +563,7 @@
             kw[:, k : k + 1536] = w
             s = tile_sum(w * w)
             acc = s if acc is None else acc + s
+            token_gram(k // 1536 + 1)
             yield
         arv[1, 0, 0] = acc
 
@@ -572,21 +578,29 @@
         send(pr2.at[1, x_at(k)], pr2.at[0, x], p2_s.at[k - 1], p2_r.at[k - 1], x_peer(k))
         for k in range(1, N_X)
     ]
+    sums = [None, None]
+    for b in range(N_X):
+        cols = pl.ds(b * PAD, PAD)
+        for j, other in enumerate((pt1, ptx)):
+            t = tile_sum(other[:, cols] * pr2[1, b].astype(f32))
+            sums[j] = t if sums[j] is None else sums[j] + t
+    for j in range(2):
+        arv[1, 0, 1 + j] = sums[j]
     wait_all(cps)
-    own = pr2[0].reshape(TOK, PAD).T
-    sums = [None, None, None]
-    for k in range(0, D, 512):
-        cols = slice(k, k + 512)
-        acc = dot(own, X[:, cols])[0:ROWS, :]
-        k2[:, cols] = acc
-        for j, other in enumerate((start[:, cols], kw[:, cols], acc)):
-            s = tile_sum(other * acc)
-            sums[j] = s if sums[j] is None else sums[j] + s
-    for j in range(3):
-        arv[1, 0, 1 + j] = sums[j]
-    out_2 = pltpu.make_async_copy(k2, k2_hbm, out_sem.at[1])
-    out_2.start()
-    run(all_sum(1, 4))
+    own = pr2[0].reshape(TOK, PAD)
+    arv[1, 0, 3] = tile_sum((dot(g_hi[...], own) + dot(g_lo[...], own)) * own.astype(f32))
+    outs = [out_w]
+
+    def image_two():
+        turned = own.T
+        for k in range(0, D, 512):
+            k2[:, k : k + 512] = dot(turned, X[:, k : k + 512])[0:ROWS, :]
+            if k == 2048:
+                yield
+        outs.append(pltpu.make_async_copy(k2, k2_hbm, out_sem.at[1]))
+        outs[1].start()
+
+    run(all_sum(1, 4), image_two())
     ww, sk, wk, kk = [jnp.sum(arv[1, 2, j], keepdims=True) / count for j in range(4)]
     sq1 = s1 * s1 * ww
     scale2 = lax.rsqrt(sq1 + norm_eps)
@@ -606,8 +620,8 @@
     results = (h11, h12, h22, jnp.sqrt(sq1), jnp.sqrt(sq2), s2, s3 * s2, -s3 * h12 * s1, -s3 * h22 * s2)
     for j, value in enumerate(results):
         mix[j] = value[0, 0]
-    out_w.wait()
-    out_2.wait()
+    for cp in outs:
+        cp.wait()
     settle(0)
 
 
@@ -646,16 +660,17 @@
 def per_device(hidden_in, targets, norm_gain, up_weight, down_weight, start):
     vm, dma = pltpu.VMEM, pltpu.SemaphoreType.DMA
     any_spec = pl.BlockSpec(memory_space=pl.ANY)
-    vmem_spec = pl.BlockSpec(memory_space=pltpu.VMEM)
     smem_spec = pl.BlockSpec(memory_space=pltpu.SMEM)
     scratch = [
+        vm((OWN, D), bf16),
+        vm((OWN, D), bf16),
+        vm((D,), f32),
         vm((HID, D), bf16),
         vm((HID, D), bf16),
         vm((ROWS, D), f32),
         vm((HID, D), bf16),
         vm((TOK, D), bf16),
         vm((CHUNKS, N_Z, OWN, W), bf16),
-        vm((BLK, D), f32),
         vm((2, GRP, D), f32),
         vm((3, CHUNKS, 3, BLK, W), bf16),
         vm((3, CHUNKS, 3, BLK, W), bf16),
@@ -675,15 +690,15 @@
         vm((GRP, HID), f32),
         vm((TOK, HID), bf16),
         vm((2, N_X, GRP, PAD), bf16),
-        vm((GRP, TOK), bf16),
-        vm((GRP, TOK), bf16),
+        vm((TOK, TOK), bf16),
+        vm((TOK, TOK), bf16),
         vm((ROWS, D), f32),
         vm((ROWS, D), f32),
         vm((2, 3, 4, 8, 128), f32),
         vm((2, 2, 15, 4, 8, 128), f32),
         vm((3, OWN, D), f32),
         vm((OWN, D), f32),
-        dma((2 * N_X + 1,)),
+        dma((2 * N_X + 4,)),
     ]
     pairs = [
         (CHUNKS,), (CHUNKS, 6), (CHUNKS, 4),
@@ -702,7 +717,7 @@
             jax.ShapeDtypeStruct((ROWS, D), f32),
             jax.ShapeDtypeStruct((9,), f32),
         ),
-        in_specs=[vmem_spec, vmem_spec, vmem_spec, any_spec, any_spec, any_spec],
+        in_specs=[any_spec] * 6,
         out_specs=(any_spec, any_spec, smem_spec),
         scratch_shapes=scratch,
         compiler_params=pltpu.CompilerParams(

time: 154 us -> 152 us (0.987)
  Pallas kernels: 153 us -> 151 us
    pallas_call x1, Pallas kernels: 148 us -> 146 us  [per_device(): pl.pallas_call(kernel, out_shape=(jax.ShapeDtypeStruct((ROWS, D), f32), j...]
where the time goes in v6:
time: 152 us
  Pallas kernels  151 us (99%)
    pallas_call x1, Pallas kernels, per_device(): pl.pallas_call(kernel, out_shape=(jax.ShapeDtypeStruct((ROWS, D), f32), j...  146 us
    pallas_call x1, Pallas kernels, per_device(): pl.pallas_call(combine, out_shape=(jax.ShapeDtypeStruct((2, ROWS, D), f32...  5.05 us

profile of v6, /device:TPU:1, one launch (start us, length us, event | category | flops | bytes accessed | tf_op | source)
XLA Modules:
  0.0 151.8 jit_solution(3053115846502779164)
XLA Ops:
  0.6 146.0 %shard_map.85 = (f32[96,4608]{1,0:T(8,128)}, f32[96,4608]{1,0:T(8,128)}, f32[9]{0:T(128)}) custom-call(bf16[2,4608]{1,0:T(2,128)(2,1)} %hin_hbm.1, bf16[2,4608]{1,0:T(2,128)(2,1)} %tgt_hbm.1, f32[4608]{0:T(1024)} %gain_hbm.1, bf16[384,4608]{1,0:T(8,128)(2,1)} %up_hbm.1, bf16[384,4608]{1,0:T(8,128)(2,1)} %down_hbm.1, f32[96,4608]{1,0:T(8,128)} %start_hbm.3), custom_call_target="tpu_custom_call" | custom-call | flops 5000000000 | bytes 14000000 | tf_op jit(solution)/shard_map/pallas_call | solution.py:713
  146.6 5.0 %shard_map.86 = (f32[2,96,4608]{2,1,0:T(8,128)}, f32[1]{0:T(128)}, f32[2,2]{1,0:T(2,128)}) custom-call(f32[9]{0:T(128)} %get-tuple-element.6.mix, f32[96,4608]{1,0:T(8,128)} %get-tuple-element.7.kw_hbm, f32[96,4608]{1,0:T(8,128)} %get-tuple-element.8.k2_hbm, f32[96,4608]{1,0:T(8,128)} %start_hbm.3), custom_call_target="tpu_custom_call" | custom-call | flops 10000000 | bytes 9000000 | tf_op jit(solution)/shard_map/pallas_call | solution.py:729

commit v7 on v6

--- a/solution.py
+++ b/solution.py
@@ -22,6 +22,8 @@
 OWN = BLK // N_Z
 CHUNKS = 2
 W = D // CHUNKS
+SPANS = ((0, 1536), (1536, 1280))
+XA = 2816
 KEEP = 40
 PIECE = 32
 
@@ -105,21 +107,15 @@
         pass
 
 
-def play(gens, order):
-    for j in order:
-        next(gens[j], None)
-    run(*gens)
-
-
 def kernel(
     hin_hbm, tgt_hbm, gain_hbm, up_hbm, down_hbm, start_hbm,
     kw_hbm, k2_hbm, mix,
     hin, tgt, gain, up, down, start, dirs, X, xz, part,
     sb, rc, y1b, y1r, y2b, y2r, sz, rz, az, A,
-    slope, bendag, hact, agrad, pt1, ptx,
+    slope, bendag, hact, agrad, pt1, ptx, pts, ptr,
     pfull, pr2, g_hi, g_lo, kw, k2, arv, arr, tot, bsum,
     ld_sem, xz_s, xz_r, xy_s, xy_r, xc_s, xc_r,
-    xa_s, xa_r, xac_s, xac_r, sx_s, sx_r,
+    xa_s, xa_r, xac_s, xac_r, sx_s, sx_r, xb_s, xb_r, xby_s, xby_r, xbc_s, xbc_r, pt_s, pt_r,
     rc_s, rc_r, y1_s, y1_r, y2_s, y2_r, rz_s, rz_r,
     az_s, az_r, ay_s, ay_r, ac_s, ac_r,
     pf_s, pf_r, p2_s, p2_r, ar_s, ar_r, out_sem,
@@ -407,7 +403,7 @@
             agrad[0] = agrad[0] + pre
 
     def accumulate_pt1(h, k):
-        cols = pl.ds(h * W, W)
+        cols = pl.ds(*SPANS[h])
         block = rows(x_at(k) * PAD, PAD)
         lanes = pl.ds(pl.multiple_of(x_at(k) * PAD, PAD), PAD)
         term = dot_t(X[group, cols], dirs[block, cols])
@@ -418,7 +414,7 @@
 
     def start_rows(h):
         ring = ring_gather(
-            dirs, [(lambda k: x_at(k) * PAD, ROWS)], h * W, W, x_peer, sx_s.at[h], sx_r.at[h]
+            dirs, [(lambda k: x_at(k) * PAD, ROWS)], *SPANS[h], x_peer, sx_s.at[h], sx_r.at[h]
         )
         next(ring)
         yield
@@ -431,7 +427,7 @@
         accumulate_pt1(h, 2)
 
     def other_tokens(h):
-        cols = pl.ds(h * W, W)
+        cols = pl.ds(*SPANS[h])
         passed = []
 
         def pass_on(k):
@@ -440,10 +436,40 @@
                 passed.append(send(X.at[at], X.at[at], xac_s.at[h, k % 4], xac_r.at[h, k % 4], c_peer))
 
         yield from ring_gather(
-            X, [(lambda k: x_at(k) * GRP + c * HALF, HALF)], h * W, W, x_peer, xa_s.at[h], xa_r.at[h], pass_on
+            X,
+            [(lambda k: x_at(k) * GRP + c * HALF, HALF)],
+            *SPANS[h],
+            x_peer,
+            xa_s.at[h],
+            xa_r.at[h],
+            pass_on,
         )
         yield
         wait_all(passed)
+
+    def far_tokens():
+        yield from ring_gather(
+            X, [(lambda k: x_at(k) * GRP + c * HALF + y * BLK, BLK)], XA, D - XA, x_peer, xb_s, xb_r
+        )
+        blocks = [
+            (lambda k, b=b: x_at(b) * GRP + c * HALF + y_at(k) * BLK, BLK) for b in range(1, N_X)
+        ]
+        yield from ring_gather(X, blocks, XA, D - XA, y_peer, xby_s, xby_r)
+        passed = []
+        for b in range(1, N_X):
+            at = (rows(x_at(b) * GRP + c * HALF, HALF), pl.ds(XA, D - XA))
+            passed.append(send(X.at[at], X.at[at], xbc_s.at[b], xbc_r.at[b], c_peer))
+        yield
+        wait_all(passed)
+        cols = pl.ds(XA, D - XA)
+        pts[...] = dot_t(X[:, cols], dirs[rows(x * PAD, PAD), cols])
+        ptr[x] = pts[group, :]
+        cps = [
+            send(pts.at[rows(x_at(k) * GRP, GRP)], ptr.at[x], pt_s.at[k - 1], pt_r.at[k - 1], x_peer(k))
+            for k in range(1, N_X)
+        ]
+        yield
+        wait_all(cps)
 
     def local_work():
         loads[-1].wait()
@@ -460,10 +486,12 @@
             cp.wait()
         arv[0, 0, 1] = tile_sum(start[...] * start[...])
 
-    s_gens = [start_rows(h) for h in range(CHUNKS)]
-    both = list(range(CHUNKS))
-    n = CHUNKS
-    play([group_tokens(h) for h in range(CHUNKS)] + [local_work()], both + [n] + both + [n] + both + both)
+    s_gens = [start_rows(h) for h in range(2)]
+    far = far_tokens()
+    local_work_gen = local_work()
+    toks = [group_tokens(h) for h in range(CHUNKS)]
+    for g in toks + [local_work_gen] + toks + [far, local_work_gen] + toks + [far] + toks:
+        next(g, None)
 
     def to_branch(i, h):
         for k in range(h * W, (h + 1) * W, W // 3):
@@ -485,12 +513,16 @@
         bendag[...] = bendag[...] * agrad[0]
 
     def first_tangent():
-        hact[...] = (slope[...] * pt1[...]).astype(bf16)
+        for b in range(N_X):
+            lanes = pl.ds(b * PAD, PAD)
+            whole = pt1[:, lanes] + ptr[b]
+            pt1[:, lanes] = whole
+            hact[:, lanes] = (slope[:, lanes] * whole).astype(bf16)
         yield from scatters(1, to_branch)
 
     fwd = forward()
-    others = [other_tokens(h) for h in range(CHUNKS)]
-    for g in s_gens + [fwd] + s_gens + [fwd] + s_gens + [fwd]:
+    others = [other_tokens(h) for h in range(2)]
+    for g in [far] + s_gens + [fwd, far] + s_gens + [fwd, far] + s_gens + [far, fwd, far]:
         next(g, None)
     tangent = first_tangent()
     for g in [tangent, fwd] + others:
@@ -688,6 +720,8 @@
         vm((2, GRP, HID), f32),
         vm((GRP, HID), f32),
         vm((GRP, HID), f32),
+        vm((TOK, PAD), f32),
+        vm((N_X, GRP, PAD), f32),
         vm((TOK, HID), bf16),
         vm((2, N_X, GRP, PAD), bf16),
         vm((TOK, TOK), bf16),
@@ -702,7 +736,7 @@
     ]
     pairs = [
         (CHUNKS,), (CHUNKS, 6), (CHUNKS, 4),
-        (CHUNKS, 4), (CHUNKS, 4), (CHUNKS, 4),
+        (2, 4), (2, 4), (2, 4), (4,), (12,), (4,), (N_X - 1,),
         (3, CHUNKS), (3, CHUNKS, 4), (3, CHUNKS, 2), (3, CHUNKS),
         (3, CHUNKS), (3, CHUNKS, 6), (3, CHUNKS, 4),
         (N_X - 1,), (N_X - 1,), (2, 2),

time: 152 us -> 155 us (1.020)
  Pallas kernels: 151 us -> 154 us
    pallas_call x1, Pallas kernels: 146 us -> 149 us  [per_device(): pl.pallas_call(kernel, out_shape=(jax.ShapeDtypeStruct((ROWS, D), f32), j...]
where the time goes in v7:
time: 155 us
  Pallas kernels  154 us (99%)
    pallas_call x1, Pallas kernels, per_device(): pl.pallas_call(kernel, out_shape=(jax.ShapeDtypeStruct((ROWS, D), f32), j...  149 us
    pallas_call x1, Pallas kernels, per_device(): pl.pallas_call(combine, out_shape=(jax.ShapeDtypeStruct((2, ROWS, D), f32...  5.05 us

profile of v7, /device:TPU:1, one launch (start us, length us, event | category | flops | bytes accessed | tf_op | source)
XLA Modules:
  0.0 155.2 jit_solution(4715610057965406637)
XLA Ops:
  0.6 149.3 %shard_map.85 = (f32[96,4608]{1,0:T(8,128)}, f32[96,4608]{1,0:T(8,128)}, f32[9]{0:T(128)}) custom-call(bf16[2,4608]{1,0:T(2,128)(2,1)} %hin_hbm.1, bf16[2,4608]{1,0:T(2,128)(2,1)} %tgt_hbm.1, f32[4608]{0:T(1024)} %gain_hbm.1, bf16[384,4608]{1,0:T(8,128)(2,1)} %up_hbm.1, bf16[384,4608]{1,0:T(8,128)(2,1)} %down_hbm.1, f32[96,4608]{1,0:T(8,128)} %start_hbm.3), custom_call_target="tpu_custom_call" | custom-call | flops 5000000000 | bytes 14000000 | tf_op jit(solution)/shard_map/pallas_call | solution.py:747
  150.0 5.0 %shard_map.86 = (f32[2,96,4608]{2,1,0:T(8,128)}, f32[1]{0:T(128)}, f32[2,2]{1,0:T(2,128)}) custom-call(f32[9]{0:T(128)} %get-tuple-element.6.mix, f32[96,4608]{1,0:T(8,128)} %get-tuple-element.7.kw_hbm, f32[96,4608]{1,0:T(8,128)} %get-tuple-element.8.k2_hbm, f32[96,4608]{1,0:T(8,128)} %start_hbm.3), custom_call_target="tpu_custom_call" | custom-call | flops 10000000 | bytes 9000000 | tf_op jit(solution)/shard_map/pallas_call | solution.py:763

commit v8 on v6

--- a/solution.py
+++ b/solution.py
@@ -50,23 +50,13 @@
     normed = summed * r
     pull = (normed * gain - target) * gain
     mean = jnp.sum(pull * normed, axis=-1, keepdims=True) / D
-    return r, normed, pull, mean
-
-
-def loss_grad(summed, target, gain):
-    r, normed, pull, mean = loss_parts(summed, target, gain)
-    return r * (pull - normed * mean) / float(TOK)
-
-
-def loss_curv(summed, tangent, target, gain):
-    r, normed, pull, mean = loss_parts(summed, target, gain)
-    along = jnp.sum(normed * tangent, axis=-1, keepdims=True) / D
-    d_normed = r * (tangent - normed * along)
-    d_pull = d_normed * gain * gain
-    d_mean = jnp.sum(d_pull * normed + pull * d_normed, axis=-1, keepdims=True) / D
-    grad = r * (pull - normed * mean)
-    d_grad = r * (d_pull - d_normed * mean - normed * d_mean) - (r * along) * grad
-    return d_grad / float(TOK)
+    grad = r * (pull - normed * mean) / float(TOK)
+    mix = gain * gain * normed + pull
+    bias = jnp.sum(mix * normed, axis=-1, keepdims=True) / D
+    scale = r * r * (gain * gain - mean) / float(TOK)
+    along = -(scale * normed + r * grad)
+    across = -r * normed / float(TOK)
+    return grad, normed, mix, scale, along, across, r, bias
 
 
 def dot_t(a, b):
@@ -117,7 +107,7 @@
     hin, tgt, gain, up, down, start, dirs, X, xz, part,
     sb, rc, y1b, y1r, y2b, y2r, sz, rz, az, A,
     slope, bendag, hact, agrad, pt1, ptx,
-    pfull, pr2, g_hi, g_lo, kw, k2, arv, arr, tot, bsum,
+    pfull, pr2, g_hi, g_lo, kw, k2, arv, arr, tot, bsum, lin,
     ld_sem, xz_s, xz_r, xy_s, xy_r, xc_s, xc_r,
     xa_s, xa_r, xac_s, xac_r, sx_s, sx_r,
     rc_s, rc_r, y1_s, y1_r, y2_s, y2_r, rz_s, rz_r,
@@ -269,14 +259,14 @@
     def gather(own, i, h):
         c0, out = h * W, A.at[i]
         cols = pl.ds(c0, W)
-        cps = gather_z(own[:, c0 : c0 + W], az.at[i, h], az_s.at[i, h], az_r.at[i, h])
+        cps = gather_z(own(slice(c0, c0 + W)), az.at[i, h], az_s.at[i, h], az_r.at[i, h])
         yield
         wait_all(cps)
         out[rows(c * HALF + y * BLK, BLK), cols] = join16(az.at[i, h])
         passed = []
 
         def pass_on(k):
-            if k != 2:
+            if k != 2 or i == 0:
                 at = (rows(c * HALF + y_at(k) * BLK, BLK), cols)
                 passed.append(send(out.at[at], out.at[at], ac_s.at[i, h, k % 4], ac_r.at[i, h, k % 4], c_peer))
 
@@ -289,8 +279,10 @@
             ay_s.at[i, h],
             ay_r.at[i, h],
             pass_on,
-            cross_peer,
+            cross_peer if i else None,
         )
+        if i == 0:
+            yield
         wait_all(passed)
         part_grad = dot_t(out[:, cols], down[:, cols])
         if h == 0:
@@ -352,6 +344,11 @@
         for k in range(N_Z - 1):
             s3 = s3 + rz[i, h, k].astype(f32)
         tot[i, :, cols] = s3
+        if i > 0:
+            inner = [jnp.sum(lin[j, :, cols] * s3, axis=-1, keepdims=True) for j in range(2)]
+            inners[i] = inner if h == 0 else [p + q for p, q in zip(inners[i], inner)]
+
+    inners = [None, None, None]
 
     def scatters(i, make):
         return par(*[scatter(i, h, make) for h in range(CHUNKS)])
@@ -472,6 +469,14 @@
     def weights():
         return tgt[...].astype(f32), gain[...]
 
+    state = []
+
+    def loss_curv(tangent, inner):
+        r, bias = state
+        a = inner[0] / D
+        d = r * (inner[1] / D - a * bias)
+        return lambda at: (lin[2, :, at] * tangent(at) + a * lin[3, :, at] + d * lin[4, :, at]).astype(bf16)
+
     def forward():
         for b in range(N_X):
             cols = pl.ds(b * PAD, PAD)
@@ -481,7 +486,12 @@
             bendag[:, cols] = second
         yield from scatters(0, to_branch)
         bsum[...] = hin[...].astype(f32) + tot[0]
-        yield from gathers(loss_grad(bsum[...], *weights()).astype(bf16), 0)
+        parts = loss_parts(bsum[...], *weights())
+        for j in range(5):
+            lin[j] = parts[1 + j]
+        state.extend(parts[6:])
+        grad = parts[0].astype(bf16)
+        yield from gathers(lambda at: grad[:, at], 0)
         bendag[...] = bendag[...] * agrad[0]
 
     def first_tangent():
@@ -490,13 +500,13 @@
 
     fwd = forward()
     others = [other_tokens(h) for h in range(CHUNKS)]
-    for g in s_gens + [fwd] + s_gens + [fwd] + s_gens + [fwd]:
+    for g in [s_gens[0], fwd] + s_gens[1:] + s_gens + [fwd, fwd] + s_gens:
         next(g, None)
     tangent = first_tangent()
     for g in [tangent, fwd] + others:
         next(g, None)
     run(tangent, fwd)
-    curv = loss_curv(bsum[...], tot[1], *weights())
+    curv = loss_curv(lambda at: tot[1, :, at], inners[1])
 
     def token_gram(k):
         mine = rows(x_at(k) * GRP, GRP)
@@ -505,7 +515,7 @@
         g_hi[mine, :] = hi
         g_lo[mine, :] = (g - hi.astype(f32)).astype(bf16)
 
-    grads = gathers(curv.astype(bf16), 1)
+    grads = gathers(curv, 1)
     for g in [grads] + others + [grads] + others + [grads] + others + [grads]:
         next(g, None)
     token_gram(0)
@@ -553,7 +563,9 @@
     ss = jnp.sum(arv[0, 2, 1], keepdims=True) / count
     s1 = lax.rsqrt(ss + norm_eps)
     h11 = s1 * s1 * q
-    curv = loss_curv(bsum[...], tot[2] - h11 * tot[1], *weights())
+    curv = loss_curv(
+        lambda at: tot[2, :, at] - h11 * tot[1, :, at], [p - h11 * q for p, q in zip(inners[2], inners[1])]
+    )
 
     def remainder():
         ptx[...] = ptx[...] - h11 * pt1[...]
@@ -567,7 +579,7 @@
             yield
         arv[1, 0, 0] = acc
 
-    run(gathers(curv.astype(bf16), 2), remainder())
+    run(gathers(curv, 2), remainder())
     out_w = pltpu.make_async_copy(kw, kw_hbm, out_sem.at[0])
     out_w.start()
     for b in range(N_X):
@@ -698,6 +710,7 @@
         vm((2, 2, 15, 4, 8, 128), f32),
         vm((3, OWN, D), f32),
         vm((OWN, D), f32),
+        vm((5, OWN, D), f32),
         dma((2 * N_X + 4,)),
     ]
     pairs = [

time: 152 us -> 147 us (0.967)
  Pallas kernels: 151 us -> 147 us
    pallas_call x1, Pallas kernels: 146 us -> 141 us  [per_device(): pl.pallas_call(kernel, out_shape=(jax.ShapeDtypeStruct((ROWS, D), f32), j...]
where the time goes in v8:
time: 147 us
  Pallas kernels  147 us (100%)
    pallas_call x1, Pallas kernels, per_device(): pl.pallas_call(kernel, out_shape=(jax.ShapeDtypeStruct((ROWS, D), f32), j...  141 us
    pallas_call x1, Pallas kernels, per_device(): pl.pallas_call(combine, out_shape=(jax.ShapeDtypeStruct((2, ROWS, D), f32...  5.05 us

profile of v8, /device:TPU:1, one launch (start us, length us, event | category | flops | bytes accessed | tf_op | source)
XLA Modules:
  0.0 147.3 jit_solution(16652571512200996744)
XLA Ops:
  0.6 141.5 %shard_map.85 = (f32[96,4608]{1,0:T(8,128)}, f32[96,4608]{1,0:T(8,128)}, f32[9]{0:T(128)}) custom-call(bf16[2,4608]{1,0:T(2,128)(2,1)} %hin_hbm.1, bf16[2,4608]{1,0:T(2,128)(2,1)} %tgt_hbm.1, f32[4608]{0:T(1024)} %gain_hbm.1, bf16[384,4608]{1,0:T(8,128)(2,1)} %up_hbm.1, bf16[384,4608]{1,0:T(8,128)(2,1)} %down_hbm.1, f32[96,4608]{1,0:T(8,128)} %start_hbm.3), custom_call_target="tpu_custom_call" | custom-call | flops 5000000000 | bytes 14000000 | tf_op jit(solution)/shard_map/pallas_call | solution.py:726
  142.1 5.0 %shard_map.86 = (f32[2,96,4608]{2,1,0:T(8,128)}, f32[1]{0:T(128)}, f32[2,2]{1,0:T(2,128)}) custom-call(f32[9]{0:T(128)} %get-tuple-element.6.mix, f32[96,4608]{1,0:T(8,128)} %get-tuple-element.7.kw_hbm, f32[96,4608]{1,0:T(8,128)} %get-tuple-element.8.k2_hbm, f32[96,4608]{1,0:T(8,128)} %start_hbm.3), custom_call_target="tpu_custom_call" | custom-call | flops 10000000 | bytes 9000000 | tf_op jit(solution)/shard_map/pallas_call | solution.py:742

commit v9 on v8

--- a/solution.py
+++ b/solution.py
@@ -88,6 +88,18 @@
                 gens.remove(g)
         if gens:
             yield
+
+
+def loop(count, body):
+    def step(k, carry):
+        body(k)
+        return carry
+
+    lax.fori_loop(0, count, step, 0)
+
+
+def span(k, size):
+    return pl.ds(pl.multiple_of(k * size, size), size)
 
 
 def run(*gens):
@@ -256,6 +268,14 @@
     def join16(buf):
         return buf[...].reshape(BLK, W)
 
+    def by_hidden(tokens, weight, cols, out, fresh):
+        def body(k):
+            hid = span(k, 2 * PAD)
+            term = dot_t(tokens, weight[hid, cols])
+            out[:, hid] = term if fresh else out[:, hid] + term
+
+        loop(HID // (2 * PAD), body)
+
     def gather(own, i, h):
         c0, out = h * W, A.at[i]
         cols = pl.ds(c0, W)
@@ -284,11 +304,7 @@
         if i == 0:
             yield
         wait_all(passed)
-        part_grad = dot_t(out[:, cols], down[:, cols])
-        if h == 0:
-            agrad[i % 2] = part_grad
-        else:
-            agrad[i % 2] = agrad[i % 2] + part_grad
+        by_hidden(out[:, cols], down, cols, agrad.at[i % 2], h == 0)
 
     def scatter(i, h, make):
         c0 = h * W
@@ -397,21 +413,13 @@
             cross_peer,
         )
         wait_all(passed)
-        pre = dot_t(X[group, cols], up[:, cols])
-        if h == 0:
-            agrad[0] = pre
-        else:
-            agrad[0] = agrad[0] + pre
+        by_hidden(X[group, cols], up, cols, agrad.at[0], h == 0)
 
     def accumulate_pt1(h, k):
         cols = pl.ds(h * W, W)
-        block = rows(x_at(k) * PAD, PAD)
-        lanes = pl.ds(pl.multiple_of(x_at(k) * PAD, PAD), PAD)
+        block = span((x + k) % N_X, PAD)
         term = dot_t(X[group, cols], dirs[block, cols])
-        if h == 0:
-            pt1[:, lanes] = term
-        else:
-            pt1[:, lanes] = pt1[:, lanes] + term
+        pt1[:, block] = term if h == 0 else pt1[:, block] + term
 
     def start_rows(h):
         ring = ring_gather(
@@ -421,8 +429,7 @@
         yield
         next(ring)
         yield
-        for k in (0, -1, 1):
-            accumulate_pt1(h, k)
+        loop(3, lambda k: accumulate_pt1(h, k + 3))
         yield
         run(ring)
         accumulate_pt1(h, 2)
@@ -444,18 +451,30 @@
 
     def local_work():
         loads[-1].wait()
-        dirs[rows(x * PAD, ROWS), :] = start[...].astype(bf16)
+
+        def cast(k):
+            dirs[rows(x * PAD + k * 16, 16), :] = start[span(k, 16), :].astype(bf16)
+
+        loop(ROWS // 16, cast)
         for g in s_gens:
             next(g)
-        for b in range(N_X):
-            pad = pl.ds(b * PAD + ROWS, PAD - ROWS)
-            up[pad, :] = jnp.zeros((PAD - ROWS, D), bf16)
-            down[pad, :] = jnp.zeros((PAD - ROWS, D), bf16)
-            dirs[pad, :] = jnp.zeros((PAD - ROWS, D), bf16)
+
+        def clear(b):
+            pad = rows(b * PAD + ROWS, PAD - ROWS)
+            for ref in (up, down, dirs):
+                ref[pad, :] = jnp.zeros((PAD - ROWS, D), bf16)
+
+        loop(N_X, clear)
         yield
         for cp in loads[:-1]:
             cp.wait()
-        arv[0, 0, 1] = tile_sum(start[...] * start[...])
+        arv[0, 0, 1] = jnp.zeros((8, 128), f32)
+
+        def square(k):
+            v = start[span(k, 16), :]
+            arv[0, 0, 1] = arv[0, 0, 1] + tile_sum(v * v)
+
+        loop(ROWS // 16, square)
 
     s_gens = [start_rows(h) for h in range(CHUNKS)]
     both = list(range(CHUNKS))
@@ -463,8 +482,11 @@
     play([group_tokens(h) for h in range(CHUNKS)] + [local_work()], both + [n] + both + [n] + both + both)
 
     def to_branch(i, h):
-        for k in range(h * W, (h + 1) * W, W // 3):
-            part[i % 2, :, k : k + W // 3] = dot(hact[...], down[:, k : k + W // 3])
+        def body(k):
+            at = pl.ds(pl.multiple_of(h * W + k * (W // 3), 256), W // 3)
+            part[i % 2, :, at] = dot(hact[...], down[:, at])
+
+        loop(3, body)
 
     def weights():
         return tgt[...].astype(f32), gain[...]
@@ -478,12 +500,14 @@
         return lambda at: (lin[2, :, at] * tangent(at) + a * lin[3, :, at] + d * lin[4, :, at]).astype(bf16)
 
     def forward():
-        for b in range(N_X):
-            cols = pl.ds(b * PAD, PAD)
+        def body(b):
+            cols = span(b, PAD)
             value, first, second = gelu_parts(agrad[0, :, cols])
             hact[:, cols] = value.astype(bf16)
             slope[:, cols] = first
             bendag[:, cols] = second
+
+        loop(N_X, body)
         yield from scatters(0, to_branch)
         bsum[...] = hin[...].astype(f32) + tot[0]
         parts = loss_parts(bsum[...], *weights())
@@ -509,11 +533,16 @@
     curv = loss_curv(lambda at: tot[1, :, at], inners[1])
 
     def token_gram(k):
-        mine = rows(x_at(k) * GRP, GRP)
-        g = dot_t(X[mine, :], X[...])
-        hi = g.astype(bf16)
-        g_hi[mine, :] = hi
-        g_lo[mine, :] = (g - hi.astype(f32)).astype(bf16)
+        mine = span((x + k) % N_X, GRP)
+
+        def body(j):
+            at = span(j, 256)
+            g = dot_t(X[mine, :], X[at, :])
+            hi = g.astype(bf16)
+            g_hi[mine, at] = hi
+            g_lo[mine, at] = (g - hi.astype(f32)).astype(bf16)
+
+        loop(TOK // 256, body)
 
     grads = gathers(curv, 1)
     for g in [grads] + others + [grads] + others + [grads] + others + [grads]:
@@ -550,12 +579,17 @@
 
     hact[...] = (slope[...] * ptx[...]).astype(bf16)
 
+    def image(factor, out):
+        def body(k):
+            at = span(k, 512)
+            out[:, at] = dot(factor, X[:, at])[0:ROWS, :]
+
+        loop(D // 512, body)
+
     def image_one():
         own = pfull[:, pl.ds(pl.multiple_of(x * PAD, PAD), PAD)].T
-        for k in range(0, D, 512):
-            kw[:, k : k + 512] = dot(own, X[:, k : k + 512])[0:ROWS, :]
-            if k % 1536 == 1024:
-                yield
+        image(own, kw)
+        yield
 
     run(scatters(2, to_branch), all_sum(0, 2), image_one())
     count = float(ROWS * 256 * D)
@@ -569,15 +603,18 @@
 
     def remainder():
         ptx[...] = ptx[...] - h11 * pt1[...]
-        acc = None
-        for k in range(0, D, 1536):
-            w = kw[:, k : k + 1536] - h11 * start[:, k : k + 1536]
-            kw[:, k : k + 1536] = w
-            s = tile_sum(w * w)
-            acc = s if acc is None else acc + s
-            token_gram(k // 1536 + 1)
-            yield
-        arv[1, 0, 0] = acc
+        arv[1, 0, 0] = jnp.zeros((8, 128), f32)
+
+        def body(k):
+            at = span(k, 512)
+            w = kw[:, at] - h11 * start[:, at]
+            kw[:, at] = w
+            arv[1, 0, 0] = arv[1, 0, 0] + tile_sum(w * w)
+
+        loop(D // 512, body)
+        yield
+        loop(N_X - 1, lambda k: token_gram(k + 1))
+        yield
 
     run(gathers(curv, 2), remainder())
     out_w = pltpu.make_async_copy(kw, kw_hbm, out_sem.at[0])
@@ -600,15 +637,20 @@
         arv[1, 0, 1 + j] = sums[j]
     wait_all(cps)
     own = pr2[0].reshape(TOK, PAD)
-    arv[1, 0, 3] = tile_sum((dot(g_hi[...], own) + dot(g_lo[...], own)) * own.astype(f32))
+    arv[1, 0, 3] = jnp.zeros((8, 128), f32)
+
+    def own_square(k):
+        at = span(k, GRP)
+        near = dot(g_hi[at, :], own) + dot(g_lo[at, :], own)
+        arv[1, 0, 3] = arv[1, 0, 3] + tile_sum(near * pr2[0, k].astype(f32))
+
+    loop(N_X, own_square)
     outs = [out_w]
 
     def image_two():
         turned = own.T
-        for k in range(0, D, 512):
-            k2[:, k : k + 512] = dot(turned, X[:, k : k + 512])[0:ROWS, :]
-            if k == 2048:
-                yield
+        image(turned, k2)
+        yield
         outs.append(pltpu.make_async_copy(k2, k2_hbm, out_sem.at[1]))
         outs[1].start()
 
@@ -658,9 +700,14 @@
     for p, at in enumerate(parts):
         for cp in ins[p]:
             cp.wait()
-        w = kw[at, :]
-        out[0, at, :] = mix[5] * w
-        out[1, at, :] = mix[6] * k2[at, :] + mix[7] * start[at, :] + mix[8] * w
+
+        def body(k, p=p):
+            part = pl.ds(pl.multiple_of(p * PIECE + k * 8, 8), 8)
+            w = kw[part, :]
+            out[0, part, :] = mix[5] * w
+            out[1, part, :] = mix[6] * k2[part, :] + mix[7] * start[part, :] + mix[8] * w
+
+        loop(PIECE // 8, body)
         for j in range(2):
             cp = pltpu.make_async_copy(out.at[j, at], basis_hbm.at[j, at], out_sem.at[j, p])
             cp.start()

time: 147 us -> 152 us (1.034)
  Pallas kernels: 147 us -> 151 us
    pallas_call x1, Pallas kernels: 141 us -> 146 us  [per_device(): pl.pallas_call(kernel, out_shape=(jax.ShapeDtypeStruct((ROWS, D), f32), j...]
where the time goes in v9:
time: 152 us; the launch traced here: 151 us
  Pallas kernels  151 us (99%)
    pallas_call x1, Pallas kernels, per_device(): pl.pallas_call(kernel, out_shape=(jax.ShapeDtypeStruct((ROWS, D), f32), j...  146 us
    pallas_call x1, Pallas kernels, per_device(): pl.pallas_call(combine, out_shape=(jax.ShapeDtypeStruct((2, ROWS, D), f32...  5.04 us

profile of v9, /device:TPU:1, one launch (start us, length us, event | category | flops | bytes accessed | tf_op | source)
XLA Modules:
  0.0 151.5 jit_solution(15057967560004799387)
XLA Ops:
  0.6 145.8 %shard_map.85 = (f32[96,4608]{1,0:T(8,128)}, f32[96,4608]{1,0:T(8,128)}, f32[9]{0:T(128)}) custom-call(bf16[2,4608]{1,0:T(2,128)(2,1)} %hin_hbm.1, bf16[2,4608]{1,0:T(2,128)(2,1)} %tgt_hbm.1, f32[4608]{0:T(1024)} %gain_hbm.1, bf16[384,4608]{1,0:T(8,128)(2,1)} %up_hbm.1, bf16[384,4608]{1,0:T(8,128)(2,1)} %down_hbm.1, f32[96,4608]{1,0:T(8,128)} %start_hbm.3), custom_call_target="tpu_custom_call" | custom-call | flops 5000000000 | bytes 14000000 | tf_op jit(solution)/shard_map/pallas_call | solution.py:773
  146.4 5.0 %shard_map.86 = (f32[2,96,4608]{2,1,0:T(8,128)}, f32[1]{0:T(128)}, f32[2,2]{1,0:T(2,128)}) custom-call(f32[9]{0:T(128)} %get-tuple-element.6.mix, f32[96,4608]{1,0:T(8,128)} %get-tuple-element.7.kw_hbm, f32[96,4608]{1,0:T(8,128)} %get-tuple-element.8.k2_hbm, f32[96,4608]{1,0:T(8,128)} %start_hbm.3), custom_call_target="tpu_custom_call" | custom-call | flops 10000000 | bytes 9000000 | tf_op jit(solution)/shard_map/pallas_call | solution.py:789

commit v10 on v8

--- a/solution.py
+++ b/solution.py
@@ -20,7 +20,7 @@
 HALF = GRP // N_C
 BLK = HALF // N_Y
 OWN = BLK // N_Z
-CHUNKS = 2
+CHUNKS = 3
 W = D // CHUNKS
 KEEP = 40
 PIECE = 32

time: 147 us -> 148 us (level)
  no operation moved by 1% of the time
where the time goes in v10:
time: 148 us; the launch traced here: 147 us
  Pallas kernels  147 us (99%)
    pallas_call x1, Pallas kernels, per_device(): pl.pallas_call(kernel, out_shape=(jax.ShapeDtypeStruct((ROWS, D), f32), j...  142 us
    pallas_call x1, Pallas kernels, per_device(): pl.pallas_call(combine, out_shape=(jax.ShapeDtypeStruct((2, ROWS, D), f32...  5.05 us

profile of v10, /device:TPU:1, one launch (start us, length us, event | category | flops | bytes accessed | tf_op | source)
XLA Modules:
  0.0 147.5 jit_solution(7330806707798572089)
XLA Ops:
  0.6 141.6 %shard_map.85 = (f32[96,4608]{1,0:T(8,128)}, f32[96,4608]{1,0:T(8,128)}, f32[9]{0:T(128)}) custom-call(bf16[2,4608]{1,0:T(2,128)(2,1)} %hin_hbm.1, bf16[2,4608]{1,0:T(2,128)(2,1)} %tgt_hbm.1, f32[4608]{0:T(1024)} %gain_hbm.1, bf16[384,4608]{1,0:T(8,128)(2,1)} %up_hbm.1, bf16[384,4608]{1,0:T(8,128)(2,1)} %down_hbm.1, f32[96,4608]{1,0:T(8,128)} %start_hbm.3), custom_call_target="tpu_custom_call" | custom-call | flops 5000000000 | bytes 14000000 | tf_op jit(solution)/shard_map/pallas_call | solution.py:726
  142.3 5.0 %shard_map.86 = (f32[2,96,4608]{2,1,0:T(8,128)}, f32[1]{0:T(128)}, f32[2,2]{1,0:T(2,128)}) custom-call(f32[9]{0:T(128)} %get-tuple-element.6.mix, f32[96,4608]{1,0:T(8,128)} %get-tuple-element.7.kw_hbm, f32[96,4608]{1,0:T(8,128)} %get-tuple-element.8.k2_hbm, f32[96,4608]{1,0:T(8,128)} %start_hbm.3), custom_call_target="tpu_custom_call" | custom-call | flops 10000000 | bytes 9000000 | tf_op jit(solution)/shard_map/pallas_call | solution.py:742

commit v11 on v10

--- a/solution.py
+++ b/solution.py
@@ -505,7 +505,9 @@
     tangent = first_tangent()
     for g in [tangent, fwd] + others:
         next(g, None)
-    run(tangent, fwd)
+    for g in [tangent, fwd, tangent, fwd, others[0]]:
+        next(g, None)
+    run(tangent)
     curv = loss_curv(lambda at: tot[1, :, at], inners[1])
 
     def token_gram(k):
@@ -516,8 +518,9 @@
         g_lo[mine, :] = (g - hi.astype(f32)).astype(bf16)
 
     grads = gathers(curv, 1)
-    for g in [grads] + others + [grads] + others + [grads] + others + [grads]:
+    for g in [grads, fwd, *others[1:], fwd, grads, others[0], grads, *others[1:], *others]:
         next(g, None)
+    run(fwd, *others)
     token_gram(0)
     run(grads)
     p1 = agrad[1] * slope[...] + bendag[...] * pt1[...]
@@ -557,12 +560,18 @@
             if k % 1536 == 1024:
                 yield
 
-    run(scatters(2, to_branch), all_sum(0, 2), image_one())
     count = float(ROWS * 256 * D)
-    q = jnp.sum(arv[0, 2, 0], keepdims=True) / count
-    ss = jnp.sum(arv[0, 2, 1], keepdims=True) / count
-    s1 = lax.rsqrt(ss + norm_eps)
-    h11 = s1 * s1 * q
+    firsts = []
+
+    def first_sums():
+        yield from all_sum(0, 2)
+        q = jnp.sum(arv[0, 2, 0], keepdims=True) / count
+        ss = jnp.sum(arv[0, 2, 1], keepdims=True) / count
+        s1 = lax.rsqrt(ss + norm_eps)
+        firsts.extend([q, ss, s1, s1 * s1 * q])
+
+    run(scatters(2, to_branch), first_sums(), image_one())
+    q, ss, s1, h11 = firsts
     curv = loss_curv(
         lambda at: tot[2, :, at] - h11 * tot[1, :, at], [p - h11 * q for p, q in zip(inners[2], inners[1])]
     )

time: 148 us -> 142 us (0.959)
  Pallas kernels: 147 us -> 142 us
    pallas_call x1, Pallas kernels: 142 us -> 136 us  [per_device(): pl.pallas_call(kernel, out_shape=(jax.ShapeDtypeStruct((ROWS, D), f32), j...]
where the time goes in v11:
time: 142 us
  Pallas kernels  142 us (100%)
    pallas_call x1, Pallas kernels, per_device(): pl.pallas_call(kernel, out_shape=(jax.ShapeDtypeStruct((ROWS, D), f32), j...  136 us
    pallas_call x1, Pallas kernels, per_device(): pl.pallas_call(combine, out_shape=(jax.ShapeDtypeStruct((2, ROWS, D), f32...  5.05 us

profile of v11, /device:TPU:1, one launch (start us, length us, event | category | flops | bytes accessed | tf_op | source)
XLA Modules:
  0.0 142.3 jit_solution(150089041385502936)
XLA Ops:
  0.6 136.5 %shard_map.85 = (f32[96,4608]{1,0:T(8,128)}, f32[96,4608]{1,0:T(8,128)}, f32[9]{0:T(128)}) custom-call(bf16[2,4608]{1,0:T(2,128)(2,1)} %hin_hbm.1, bf16[2,4608]{1,0:T(2,128)(2,1)} %tgt_hbm.1, f32[4608]{0:T(1024)} %gain_hbm.1, bf16[384,4608]{1,0:T(8,128)(2,1)} %up_hbm.1, bf16[384,4608]{1,0:T(8,128)(2,1)} %down_hbm.1, f32[96,4608]{1,0:T(8,128)} %start_hbm.3), custom_call_target="tpu_custom_call" | custom-call | flops 5000000000 | bytes 14000000 | tf_op jit(solution)/shard_map/pallas_call | solution.py:735
  137.1 5.0 %shard_map.86 = (f32[2,96,4608]{2,1,0:T(8,128)}, f32[1]{0:T(128)}, f32[2,2]{1,0:T(2,128)}) custom-call(f32[9]{0:T(128)} %get-tuple-element.6.mix, f32[96,4608]{1,0:T(8,128)} %get-tuple-element.7.kw_hbm, f32[96,4608]{1,0:T(8,128)} %get-tuple-element.8.k2_hbm, f32[96,4608]{1,0:T(8,128)} %start_hbm.3), custom_call_target="tpu_custom_call" | custom-call | flops 10000000 | bytes 9000000 | tf_op jit(solution)/shard_map/pallas_call | solution.py:751

commit v12 on v11

--- a/solution.py
+++ b/solution.py
@@ -503,9 +503,7 @@
     for g in [s_gens[0], fwd] + s_gens[1:] + s_gens + [fwd, fwd] + s_gens:
         next(g, None)
     tangent = first_tangent()
-    for g in [tangent, fwd] + others:
-        next(g, None)
-    for g in [tangent, fwd, tangent, fwd, others[0]]:
+    for g in [tangent, *others, tangent, fwd, tangent, fwd, others[0]]:
         next(g, None)
     run(tangent)
     curv = loss_curv(lambda at: tot[1, :, at], inners[1])
@@ -518,7 +516,7 @@
         g_lo[mine, :] = (g - hi.astype(f32)).astype(bf16)
 
     grads = gathers(curv, 1)
-    for g in [grads, fwd, *others[1:], fwd, grads, others[0], grads, *others[1:], *others]:
+    for g in [grads, fwd, *others[1:], fwd, grads, others[0], fwd, grads, *others[1:], *others]:
         next(g, None)
     run(fwd, *others)
     token_gram(0)

time: 142 us -> 142 us (level)
  no operation moved by 1% of the time
where the time goes in v12:
time: 142 us
  Pallas kernels  141 us (99%)
    pallas_call x1, Pallas kernels, per_device(): pl.pallas_call(kernel, out_shape=(jax.ShapeDtypeStruct((ROWS, D), f32), j...  136 us
    pallas_call x1, Pallas kernels, per_device(): pl.pallas_call(combine, out_shape=(jax.ShapeDtypeStruct((2, ROWS, D), f32...  5.05 us

profile of v12, /device:TPU:1, one launch (start us, length us, event | category | flops | bytes accessed | tf_op | source)
XLA Modules:
  0.0 142.1 jit_solution(539864875956239773)
XLA Ops:
  0.6 136.3 %shard_map.85 = (f32[96,4608]{1,0:T(8,128)}, f32[96,4608]{1,0:T(8,128)}, f32[9]{0:T(128)}) custom-call(bf16[2,4608]{1,0:T(2,128)(2,1)} %hin_hbm.1, bf16[2,4608]{1,0:T(2,128)(2,1)} %tgt_hbm.1, f32[4608]{0:T(1024)} %gain_hbm.1, bf16[384,4608]{1,0:T(8,128)(2,1)} %up_hbm.1, bf16[384,4608]{1,0:T(8,128)(2,1)} %down_hbm.1, f32[96,4608]{1,0:T(8,128)} %start_hbm.3), custom_call_target="tpu_custom_call" | custom-call | flops 5000000000 | bytes 14000000 | tf_op jit(solution)/shard_map/pallas_call | solution.py:733
  136.9 5.0 %shard_map.86 = (f32[2,96,4608]{2,1,0:T(8,128)}, f32[1]{0:T(128)}, f32[2,2]{1,0:T(2,128)}) custom-call(f32[9]{0:T(128)} %get-tuple-element.6.mix, f32[96,4608]{1,0:T(8,128)} %get-tuple-element.7.kw_hbm, f32[96,4608]{1,0:T(8,128)} %get-tuple-element.8.k2_hbm, f32[96,4608]{1,0:T(8,128)} %start_hbm.3), custom_call_target="tpu_custom_call" | custom-call | flops 10000000 | bytes 9000000 | tf_op jit(solution)/shard_map/pallas_call | solution.py:749
